TPU v7x, 32 devices: a whole 2x2x4 slice. The times are simulated.
32 devices in a mesh: groups: 2 (over y), expert: 4 (over z), dp: 4 (over x, core).
Axes of the slice: x: 2, y: 2, z: 4, core: 2. Of those that a mesh axis runs over, the one named last changes fastest.
Arguments:
- tokens: bfloat16 [2048, 7168], P(('groups', 'expert'), 'dp'), parts along dimension 0, may hold values from -6 to 6
- cotangent: bfloat16 [2048, 7168], P(('groups', 'expert'), 'dp'), parts along dimension 0, may hold values from -6 to 6
- expert_ids: int32 [2048, 8], P(('groups', 'expert')), parts along dimension 0, may hold values from 0 to 255, as said below
- gate_values: bfloat16 [2048, 8], P(('groups', 'expert')), parts along dimension 0, may hold values from 0.049804688 to 1
- w_gate: bfloat16 [7168, 8192], P('dp', 'expert'), may hold values from -0.0625 to 0.0625
- w_up: bfloat16 [7168, 8192], P('dp', 'expert'), may hold values from -0.0625 to 0.0625
- w_down: bfloat16 [7168, 8192], P('dp', 'expert'), may hold values from -0.125 to 0.125
Outputs:
- output: bfloat16 [2048, 7168], P(('groups', 'expert'), 'dp'), parts along dimension 0
- input_grad: bfloat16 [2048, 7168], P(('groups', 'expert'), 'dp'), parts along dimension 0
- gate_grad: bfloat16 [2048, 8], P(('groups', 'expert')), parts along dimension 0
- grad_gate: bfloat16 [14336, 8192], P(('groups', 'dp'), 'expert'), parts along dimension 0
- grad_up: bfloat16 [14336, 8192], P(('groups', 'dp'), 'expert'), parts along dimension 0
- grad_down: bfloat16 [14336, 8192], P(('groups', 'dp'), 'expert'), parts along dimension 0
There are 2 independent parts, one for each index of `groups`. A program takes and returns all parts, laid end to end along the dimension named above; an argument that names none is the same for every part. Nothing has to cross between parts.
Inputs may be any that keep to these rules, and one draw needn't show every extreme that they name: `expert_ids`: each row names 8 different experts. Of the experts 0 to 3, each is named by 1 to 24 of the rows of one aligned block of 256 rows; in every draw one of them is named by exactly 24 rows in every block.
All inputs are finite; a program needn't handle non-finite values.
Results may differ from a plain program's by a relative error of at most 0.0063.
Values may be sent and summed in bfloat16 or wider, within the bound.
No kernel may reach another device: no remote copies, remote signals or barrier semaphores. Data moves between devices by JAX's collectives and lax.ppermute only.
A program may use at most 192 MiB of HBM per device.

v0:
```python
import jax
import jax.numpy as jnp
from jax import lax
from jax.sharding import PartitionSpec as P

EXPERTS = 4
CAP = 24


def slot_table(expert_ids, experts, capacity):
    count = expert_ids.shape[0]
    labels = jnp.arange(experts, dtype=jnp.int32)
    member = jnp.any(expert_ids[:, :, None] == labels[None, None, :], axis=1).astype(jnp.int32)
    slot = jnp.cumsum(member, axis=0) - member
    places = jnp.arange(capacity, dtype=jnp.int32)
    chosen = member[:, :, None] * (slot[:, :, None] == places[None, None, :]).astype(jnp.int32)
    position = jnp.arange(count, dtype=jnp.int32)[:, None, None]
    filled = jnp.sum(chosen, axis=0)
    index = jnp.sum(chosen * position, axis=0) + count * (1 - filled)
    return (member, slot, index)


def expert_weights(expert_ids, gate_values, experts):
    labels = jnp.arange(experts, dtype=jnp.int32)
    match = expert_ids[:, :, None] == labels[None, None, :]
    return jnp.sum(
        jnp.where(match, gate_values.astype(jnp.float32)[:, :, None], jnp.float32(0.0)), axis=1
    )


def swiglu_grads(hidden_grad, gate, up):
    sigma = jax.nn.sigmoid(gate)
    active = gate * sigma
    d_up = (hidden_grad * active).astype(jnp.bfloat16)
    d_gate = (hidden_grad * up * sigma * (1.0 + gate * (1.0 - sigma))).astype(jnp.bfloat16)
    return (d_gate, d_up)


def contract_last(left, right):
    return lax.dot_general(
        left, right, (((1,), (1,)), ((), ())), preferred_element_type=jnp.float32
    )


def contract_first(left, right):
    return lax.dot_general(
        left, right, (((0,), (0,)), ((), ())), preferred_element_type=jnp.float32
    )


def per_device(tokens, cotangent, expert_ids, gate_values, w_gate, w_up, w_down):
    devices = lax.axis_size("expert")
    span = devices // EXPERTS
    count, width = tokens.shape
    member, slot, index = slot_table(expert_ids, EXPERTS, CAP)
    weight = expert_weights(expert_ids, gate_values, EXPERTS)
    padded_x = jnp.concatenate([tokens, jnp.zeros((1, width), tokens.dtype)], axis=0)
    padded_dy = jnp.concatenate([cotangent, jnp.zeros((1, width), cotangent.dtype)], axis=0)
    padded_w = jnp.concatenate([weight, jnp.zeros((1, EXPERTS), jnp.float32)], axis=0)
    slot_weight = jnp.take_along_axis(padded_w, index.T, axis=0).T
    pack_x = padded_x[index]
    pack_g = (slot_weight[:, :, None] * padded_dy[index].astype(jnp.float32)).astype(jnp.bfloat16)
    recv_x, recv_g = (
        lax.all_to_all(
            jnp.repeat(pack_x, span, axis=0), "expert", split_axis=0, concat_axis=0, tiled=True
        ),
        lax.all_to_all(
            jnp.repeat(pack_g, span, axis=0), "expert", split_axis=0, concat_axis=0, tiled=True
        ),
    )
    rows = recv_x.reshape(-1, width)
    grads = recv_g.reshape(-1, width)
    proj_gate = jnp.dot(rows, w_gate, preferred_element_type=jnp.float32)
    proj_up = jnp.dot(rows, w_up, preferred_element_type=jnp.float32)
    gate, up = lax.psum((proj_gate, proj_up), "dp")
    hidden = (jax.nn.silu(gate) * up).astype(jnp.bfloat16)
    hidden_grad = lax.psum(jnp.dot(grads, w_down, preferred_element_type=jnp.float32), "dp")
    d_gate, d_up = swiglu_grads(hidden_grad, gate, up)
    partial_out = contract_last(hidden, w_down).astype(jnp.bfloat16)
    input_part = (contract_last(d_gate, w_gate) + contract_last(d_up, w_up)).astype(jnp.bfloat16)
    grad_gate = contract_first(rows, d_gate).astype(jnp.bfloat16)
    grad_up = contract_first(rows, d_up).astype(jnp.bfloat16)
    grad_down = contract_first(grads, hidden).astype(jnp.bfloat16)
    back_out, back_in = (
        lax.all_to_all(
            partial_out.reshape(devices, CAP, width),
            "expert",
            split_axis=0,
            concat_axis=0,
            tiled=True,
        ),
        lax.all_to_all(
            input_part.reshape(devices, CAP, width),
            "expert",
            split_axis=0,
            concat_axis=0,
            tiled=True,
        ),
    )
    expert_out = jnp.sum(back_out.reshape(EXPERTS, span, CAP, width).astype(jnp.float32), axis=1)
    expert_in = jnp.sum(back_in.reshape(EXPERTS, span, CAP, width).astype(jnp.float32), axis=1)
    pad_rows = jnp.zeros((EXPERTS, 1, width), jnp.float32)
    padded_out = jnp.concatenate([expert_out, pad_rows], axis=1)
    padded_in = jnp.concatenate([expert_in, pad_rows], axis=1)
    pick = jnp.where(member > 0, slot, CAP)
    labels = jnp.arange(EXPERTS, dtype=jnp.int32)
    picked_out = padded_out[labels[None, :], pick]
    picked_in = padded_in[labels[None, :], pick]
    output = jnp.sum(weight[:, :, None] * picked_out, axis=1).astype(jnp.bfloat16)
    input_grad = jnp.sum(picked_in, axis=1).astype(jnp.bfloat16)
    scores = lax.psum(jnp.sum(cotangent.astype(jnp.float32)[:, None, :] * picked_out, axis=2), "dp")
    match = expert_ids[:, :, None] == labels[None, None, :]
    gate_grad = jnp.sum(jnp.where(match, scores[:, None, :], jnp.float32(0.0)), axis=2).astype(
        jnp.bfloat16
    )
    return (output, input_grad, gate_grad, grad_gate, grad_up, grad_down)


def solution(mesh):
    in_specs = (
        P(("groups", "expert"), "dp"),
        P(("groups", "expert"), "dp"),
        P(("groups", "expert"), None),
        P(("groups", "expert"), None),
        P("dp", "expert"),
        P("dp", "expert"),
        P("dp", "expert"),
    )
    out_specs = (
        P(("groups", "expert"), "dp"),
        P(("groups", "expert"), "dp"),
        P(("groups", "expert"), None),
        P(("groups", "dp"), "expert"),
        P(("groups", "dp"), "expert"),
        P(("groups", "dp"), "expert"),
    )
    return jax.shard_map(
        per_device, mesh=mesh, in_specs=in_specs, out_specs=out_specs, check_vma=False
    )
```

profile of v0, /device:TPU:0, one launch (start us, length us, event | category | flops | bytes accessed | tf_op | source)
XLA Modules:
  0.0 247.1 jit_solution(6623701902150606138)
XLA Ops:
  11.1 1.6 gather_fusion
  12.7 6.5 %all-to-all-start = ((bf16[4,24,1792]{2,1,0:T(8,128)(2,1)}), bf16[4,24,1792]{2,1,0:T(8,128)(2,1)S(1)}, u32[]{:S(2)}, u32[]{:S(2)}) async-start(bf16[4,24,1792]{2,1,0:T(8,128)(2,1)} %bitcast.4), calls=%async_computation | async-start | bytes 688128 | tf_op jit(solution)/shard_map/all_to_all | solution.py:64
  24.2 5.6 %all-to-all-done = bf16[4,24,1792]{2,1,0:T(8,128)(2,1)S(1)} async-done(((bf16[4,24,1792]{2,1,0:T(8,128)(2,1)}), bf16[4,24,1792]{2,1,0:T(8,128)(2,1)S(1)}, u32[]{:S(2)}, u32[]{:S(2)}) %all-to-all-start) | async-done | bytes 344096 | tf_op jit(solution)/shard_map/all_to_all | solution.py:64
  29.8 4.4 %all-to-all-start.2 = ((bf16[4,24,1792]{2,1,0:T(8,128)(2,1)}), bf16[4,24,1792]{2,1,0:T(8,128)(2,1)}, u32[]{:S(2)}, u32[]{:S(2)}) async-start(bf16[4,24,1792]{2,1,0:T(8,128)(2,1)} %fusion.2), calls=%async_computation.2 | async-start | bytes 688128 | tf_op jit(solution)/shard_map/all_to_all | solution.py:67
  34.2 5.4 %fusion.13 = f32[96,2048]{1,0:T(8,128)} fusion(bf16[96,1792]{1,0:T(8,128)(2,1)S(1)} %bitcast.64, bf16[1792,2048]{1,0:T(8,128)(2,1)} %param.11), kind=kOutput, calls=%fused_computation.50 | convolution fusion | flops 704643072 | bytes 8470528 | tf_op jit(solution)/shard_map/dot_general | solution.py:73
  39.6 2.2 fusion.14
  43.1 5.4 %fusion.15 = f32[96,2048]{1,0:T(8,128)} fusion(bf16[96,1792]{1,0:T(8,128)(2,1)} %bitcast.12, bf16[1792,2048]{1,0:T(8,128)(2,1)} %param.13), kind=kOutput, calls=%fused_computation.52 | convolution fusion | flops 704643072 | bytes 8470528 | tf_op jit(solution)/shard_map/dot_general | solution.py:77
  50.1 54.6 %all-reduce.8.cloned.1.call-done = (f32[96,2048]{1,0:T(8,128)}, f32[96,2048]{1,0:T(8,128)}, f32[96,2048]{1,0:T(8,128)}) async-done(((f32[96,2048]{1,0:T(8,128)}, f32[96,2048]{1,0:T(8,128)}, f32[96,2048]{1,0:T(8,128)}), (f32[96,2048]{1,0:T(8,128)}, f32[96,2048]{1,0:T(8,128)}, f32[96,2048]{1,0:T(8,128)})) %all-reduce.8.cloned.1.call-update) | async-done | bytes 2359312 | tf_op jit(solution)/shard_map/psum | solution.py:75
  104.8 2.0 multiply_convert_fusion
  106.8 5.6 %fusion.16 = f32[96,1792]{1,0:T(8,128)S(1)} fusion(bf16[96,2048]{1,0:T(8,128)(2,1)S(1)} %get-tuple-element.16, bf16[1792,2048]{1,0:T(8,128)(2,1)} %param.11), kind=kOutput, calls=%fused_computation.53 | convolution fusion | flops 704643072 | bytes 8421376 | tf_op jit(solution)/shard_map/dot_general | solution.py:40
  112.4 5.1 %convolution_convert_fusion.1 = bf16[1792,2048]{1,0:T(8,128)(2,1)} fusion(bf16[96,1792]{1,0:T(8,128)(2,1)S(1)} %bitcast.66, bf16[96,2048]{1,0:T(8,128)(2,1)S(1)} %get-tuple-element.15), kind=kOutput, calls=%fused_computation.6 | convolution fusion | flops 708313088 | bytes 8077312 | tf_op jit(solution)/shard_map/dot_general | solution.py:46
  117.6 3.1 %fusion = bf16[96,1792]{1,0:T(8,128)(2,1)} fusion(f32[96,1792]{1,0:T(8,128)S(1)} %fusion.16, bf16[96,2048]{1,0:T(8,128)(2,1)S(1)} %get-tuple-element.15, bf16[1792,2048]{1,0:T(8,128)(2,1)S(1)} %bitcast.63), kind=kOutput, calls=%fused_computation.12 | convolution fusion | flops 704987136 | bytes 8765440 | tf_op jit(solution)/shard_map/dot_general | solution.py:40
  120.7 4.6 %all-to-all-start.3 = ((bf16[4,24,1792]{2,1,0:T(8,128)(2,1)}), bf16[4,24,1792]{2,1,0:T(8,128)(2,1)}, u32[]{:S(2)}, u32[]{:S(2)}) async-start(bf16[4,24,1792]{2,1,0:T(8,128)(2,1)} %bitcast.69), calls=%async_computation.3 | async-start | bytes 688128 | tf_op jit(solution)/shard_map/all_to_all | solution.py:92
  125.3 6.1 %convolution_convert_fusion = bf16[1792,2048]{1,0:T(8,128)(2,1)} fusion(bf16[96,1792]{1,0:T(8,128)(2,1)} %bitcast.12, bf16[96,2048]{1,0:T(8,128)(2,1)S(1)} %get-tuple-element.17), kind=kOutput, calls=%fused_computation.5 | convolution fusion | flops 708313088 | bytes 8077312 | tf_op jit(solution)/shard_map/dot_general | solution.py:46
  131.4 6.2 %convolution_convert_fusion.3 = bf16[96,1792]{1,0:T(8,128)(2,1)} fusion(bf16[96,2048]{1,0:T(8,128)(2,1)S(1)} %get-tuple-element.17, bf16[1792,2048]{1,0:T(8,128)(2,1)} %param.13), kind=kOutput, calls=%fused_computation.11 | convolution fusion | flops 704815104 | bytes 8077312 | tf_op jit(solution)/shard_map/dot_general | solution.py:40
  137.7 5.1 %all-to-all-start.1 = ((bf16[4,24,1792]{2,1,0:T(8,128)(2,1)}), bf16[4,24,1792]{2,1,0:T(8,128)(2,1)}, u32[]{:S(2)}, u32[]{:S(2)}) async-start(bf16[4,24,1792]{2,1,0:T(8,128)(2,1)} %bitcast.68), calls=%async_computation.1 | async-start | bytes 688128 | tf_op jit(solution)/shard_map/all_to_all | solution.py:85
  142.8 5.1 %convolution_convert_fusion.2 = bf16[1792,2048]{1,0:T(8,128)(2,1)} fusion(bf16[96,1792]{1,0:T(8,128)(2,1)S(1)} %bitcast.67, bf16[96,2048]{1,0:T(8,128)(2,1)S(1)} %get-tuple-element.16), kind=kOutput, calls=%fused_computation.7 | convolution fusion | flops 708313088 | bytes 8077312 | tf_op jit(solution)/shard_map/dot_general | solution.py:46
  149.2 20.6 %gather_fusion.3 = f32[1024,1792]{1,0:T(8,128)} fusion(f32[4,25,1792]{2,0,1:T(4,128)S(1)} %pad_convert_fusion, s32[1024]{0:T(1024)S(1)} %reshape.112), kind=kCustom, calls=%fused_computation.3 | custom fusion | bytes 14688256 | tf_op jit(solution)/shard_map/gather | solution.py:108
  169.7 9.2 %reshape.129 = f32[256,4,1792]{2,1,0:T(4,128)} reshape(f32[1024,1792]{1,0:T(8,128)} %gather_fusion.3) | data formatting | bytes 14680064 | tf_op jit(solution)/shard_map/gather | solution.py:108
  179.0 8.5 %reduce_sum.75 = bf16[256,1792]{1,0:T(8,128)(2,1)} reduce(f32[256,4,1792]{2,1,0:T(4,128)} %reshape.129, f32[]{:T(128)} %constant.12.clone.1), dimensions={1}, to_apply=%region_10.11 | reduce | flops 1376256 | bytes 8257540 | tf_op jit(solution)/shard_map/reduce_sum | solution.py:110
  188.7 20.6 %gather_fusion.1 = f32[1024,1792]{1,0:T(8,128)} fusion(f32[4,25,1792]{2,0,1:T(4,128)S(1)} %pad_convert_fusion.1, s32[1024]{0:T(1024)S(1)} %reshape.112), kind=kCustom, calls=%fused_computation.1 | custom fusion | bytes 14688256 | tf_op jit(solution)/shard_map/gather | solution.py:107
  209.3 9.3 %reshape.115 = f32[256,4,1792]{2,1,0:T(4,128)} reshape(f32[1024,1792]{1,0:T(8,128)} %gather_fusion.1) | data formatting | bytes 14680064 | tf_op jit(solution)/shard_map/gather | solution.py:107
  218.6 8.9 %multiply_reduce_fusion = (f32[256,4]{1,0:T(8,128)S(1)}, bf16[256,1792]{1,0:T(8,128)(2,1)}) fusion(f32[256,4,1792]{2,1,0:T(4,128)} %reshape.115, f32[256,1792]{1,0:T(8,128)S(1)} %convert_element_type.73, f32[256,4]{1,0:T(8,128)S(1)} %copy-done.2), kind=kLoop, calls=%fused_computation.8 | loop fusion | flops 6880256 | bytes 10100736 | tf_op jit(solution)/shard_map/reduce_sum | solution.py:111
  227.5 12.1 %psum.31 = f32[256,4]{1,0:T(8,128)S(1)} all-reduce(f32[256,4]{1,0:T(8,128)S(1)} %get-tuple-element.6), channel_id=1, replica_groups=mesh['groups'=2,'expert'=4,'dp'=4] {'dp'}, use_global_device_ids=true, to_apply=%region_12.13 | all-reduce | flops 1024 | bytes 8192 | tf_op jit(solution)/shard_map/psum | solution.py:111
  (62 shorter events, 15.1 us)
Async XLA Ops:
  12.7 9.7 %copy-start = (bf16[256,1792]{1,0:T(8,128)(2,1)S(1)}, bf16[256,1792]{1,0:T(8,128)(2,1)}, u32[]{:S(2)}) copy-start(bf16[256,1792]{1,0:T(8,128)(2,1)} %param.8) | copy-start | bytes 2752516
  12.7 17.1 %all-to-all-start = ((bf16[4,24,1792]{2,1,0:T(8,128)(2,1)}), bf16[4,24,1792]{2,1,0:T(8,128)(2,1)S(1)}, u32[]{:S(2)}, u32[]{:S(2)}) async-start(bf16[4,24,1792]{2,1,0:T(8,128)(2,1)} %bitcast.4), calls=%async_computation | async-start | bytes 688128 | tf_op jit(solution)/shard_map/all_to_all | solution.py:64
  20.9 1.5 copy-start.1
  29.8 9.8 %slice-start = ((s8[7340032]{0:T(1024)(128)(4,1)}), s8[3145728]{0:T(1024)(128)(4,1)S(1)}, s32[]{:S(2)}) async-start(s8[7340032]{0:T(1024)(128)(4,1)} %bitcast.60), calls=%async_computation.5 | async-start | bytes 6291456
  29.8 13.3 %all-to-all-start.2 = ((bf16[4,24,1792]{2,1,0:T(8,128)(2,1)}), bf16[4,24,1792]{2,1,0:T(8,128)(2,1)}, u32[]{:S(2)}, u32[]{:S(2)}) async-start(bf16[4,24,1792]{2,1,0:T(8,128)(2,1)} %fusion.2), calls=%async_computation.2 | async-start | bytes 688128 | tf_op jit(solution)/shard_map/all_to_all | solution.py:67
  34.2 70.6 %all-reduce.8.cloned.1.call-start = ((), (), s32[]{:S(2)}) async-start(), calls=%async_computation.4 | async-start | bytes 4718592 | tf_op jit(solution)/shard_map/psum | solution.py:75
  34.2 5.4 %slice-start.1 = ((s8[7340032]{0:T(1024)(128)(4,1)}), s8[4194304]{0:T(1024)(128)(4,1)S(1)}, s32[]{:S(2)}) async-start(s8[7340032]{0:T(1024)(128)(4,1)} %bitcast.60), calls=%async_computation.6 | async-start | bytes 8388608
  106.8 10.8 %slice-start.2 = ((s8[7340032]{0:T(1024)(128)(4,1)}), s8[4194304]{0:T(1024)(128)(4,1)S(1)}, s32[]{:S(2)}) async-start(s8[7340032]{0:T(1024)(128)(4,1)} %bitcast.62), calls=%async_computation.7 | async-start | bytes 8388608
  112.4 5.2 %slice-start.3 = ((s8[7340032]{0:T(1024)(128)(4,1)}), s8[3145728]{0:T(1024)(128)(4,1)S(1)}, s32[]{:S(2)}) async-start(s8[7340032]{0:T(1024)(128)(4,1)} %bitcast.62), calls=%async_computation.8 | async-start | bytes 6291456
  120.7 17.0 %all-to-all-start.3 = ((bf16[4,24,1792]{2,1,0:T(8,128)(2,1)}), bf16[4,24,1792]{2,1,0:T(8,128)(2,1)}, u32[]{:S(2)}, u32[]{:S(2)}) async-start(bf16[4,24,1792]{2,1,0:T(8,128)(2,1)} %bitcast.69), calls=%async_computation.3 | async-start | bytes 688128 | tf_op jit(solution)/shard_map/all_to_all | solution.py:92
  137.7 49.8 %all-to-all-start.1 = ((bf16[4,24,1792]{2,1,0:T(8,128)(2,1)}), bf16[4,24,1792]{2,1,0:T(8,128)(2,1)}, u32[]{:S(2)}, u32[]{:S(2)}) async-start(bf16[4,24,1792]{2,1,0:T(8,128)(2,1)} %bitcast.68), calls=%async_computation.1 | async-start | bytes 688128 | tf_op jit(solution)/shard_map/all_to_all | solution.py:85
  209.3 9.3 %copy-start.2 = (f32[256,4]{1,0:T(8,128)S(1)}, f32[256,4]{1,0:T(8,128)}, u32[]{:S(2)}) copy-start(f32[256,4]{1,0:T(8,128)} %copy-done.1) | copy-start | bytes 12292
  218.6 21.0 %copy-start.3 = (s32[256,8]{0,1:T(8,128)S(1)}, s32[256,8]{0,1:T(8,128)}, u32[]{:S(2)}) copy-start(s32[256,8]{0,1:T(8,128)} %param.9) | copy-start | bytes 24580
Sparse Core Ops, SparseCore 0:
  48.7 56.0 all-reduce.7
where the time goes:
time: 248 us; the launch traced here: 247 us
  local copies, waits for them, and re-layouts  68.2 us (28%)
  waiting for transfers between devices  61.6 us (25%)
  matrix products  44.3 us (18%)
  other arithmetic  26.2 us (11%)
  starting transfers between devices  20.6 us (8%)
  between operations  14.2 us (6%)
  blocking collectives  12.1 us (5%)
    psum x1, waiting for transfers between devices, per_device(): gate, up = lax.psum((proj_gate, proj_up), 'dp')  54.6 us
    gather x2, local copies, waits for them, and re-layouts, per_device(): picked_out = padded_out[labels[None, :], pick]  29.9 us
    gather x2, local copies, waits for them, and re-layouts, per_device(): picked_in = padded_in[labels[None, :], pick]  29.8 us
    dot_general x3, matrix products, contract_first(): lax.dot_general(left, right, (((0,), (0,)), ((), ())), preferred_element_...  16.4 us
    dot_general x3, matrix products, contract_last(): lax.dot_general(left, right, (((1,), (1,)), ((), ())), preferred_element_...  14.9 us
    psum x1, blocking collectives, per_device(): lax.psum(jnp.sum(cotangent.astype(jnp.float32)[:, None, :] * picked_out,...  12.1 us
    reduce_sum x1, other arithmetic, per_device(): jnp.sum(cotangent.astype(jnp.float32)[:, None, :] * picked_out, axis=2)  8.85 us
    reduce_sum x1, other arithmetic, per_device(): input_grad = jnp.sum(picked_in, axis=1).astype(jnp.bfloat16)  8.45 us
  transfers between devices with their start and end apart: 5, of which 3 were waited for; matrix products, arithmetic and copies ran while one was open for 29% of the time, Pallas kernels for 0%

commit v1 on v0

v1 whole, which is shorter than its diff:
```python
import jax
import jax.numpy as jnp
from jax import lax
from jax.sharding import PartitionSpec as P

EXPERTS = 4
CAP = 24
BF = jnp.bfloat16
F32 = jnp.float32


def dot(left, right, dims):
    return lax.dot_general(left, right, (dims, ((), ())), preferred_element_type=F32)


def swap(value, axis, step):
    size = lax.axis_size(axis)
    return lax.ppermute(value, axis, [(i, i ^ step) for i in range(size)])


def exchange(blocks, axis):
    return [blocks[0]] + [swap(blocks[s], axis, s) for s in range(1, len(blocks))]


def halves(value, core):
    half = value.shape[1] // 2
    mine = lax.dynamic_slice_in_dim(value, core * half, half, 1)
    other = lax.dynamic_slice_in_dim(value, (1 - core) * half, half, 1)
    return mine, other


def dp_sum(values, core):
    size = lax.axis_size("dp")
    pairs = [halves(v, core) for v in values]
    got = [swap(other, "dp", 1) for _, other in pairs]
    sums = [mine + g for (mine, _), g in zip(pairs, got)]
    step = 2
    while step < size:
        got = [swap(s.astype(BF), "dp", step) for s in sums]
        sums = [s + g.astype(F32) for s, g in zip(sums, got)]
        step *= 2
    return sums


def join(mine, core):
    other = swap(mine, "dp", 1)
    first = jnp.where(core == 0, mine, other)
    second = jnp.where(core == 0, other, mine)
    return jnp.concatenate([first, second], axis=1)


def per_device(tokens, cotangent, expert_ids, gate_values, w_gate, w_up, w_down):
    devices = lax.axis_size("expert")
    span = devices // EXPERTS
    count, width = tokens.shape
    me = lax.axis_index("expert")
    core = lax.axis_index("dp") % 2
    direct = devices <= 8

    steps = jnp.arange(devices, dtype=jnp.int32)
    labels = ((steps ^ me) if direct else steps) // span
    match = expert_ids.T[None, :, :] == labels[:, None, None]
    member = jnp.any(match, axis=1)
    weight = jnp.sum(jnp.where(match, gate_values.T.astype(F32)[None], 0.0), axis=1)
    earlier = jnp.arange(count)[:, None] < jnp.arange(count)[None, :]
    slot = dot(member.astype(BF), earlier.astype(BF), ((1,), (0,)))
    places = jnp.arange(CAP, dtype=F32)
    chosen = (slot[:, None, :] == places[None, :, None]) & member[:, None, :]
    pick = chosen.astype(BF).reshape(devices * CAP, count)
    pick_w = jnp.where(chosen, weight[:, None, :], 0.0).astype(BF).reshape(devices * CAP, count)

    def move(rows):
        if direct:
            return jnp.concatenate(
                exchange([rows[s * CAP:(s + 1) * CAP] for s in range(devices)], "expert"), axis=0)
        got = lax.all_to_all(rows.reshape(devices, CAP, -1), "expert", split_axis=0, concat_axis=0, tiled=True)
        return got.reshape(devices * CAP, -1)

    rows = move(dot(pick, tokens, ((1,), (0,))).astype(BF))
    grads = move(dot(pick_w, cotangent, ((1,), (0,))).astype(BF))

    gate, up = dp_sum([dot(rows, w_gate, ((1,), (0,))), dot(rows, w_up, ((1,), (0,)))], core)
    sigma = jax.nn.sigmoid(gate)
    active = gate * sigma
    hidden_h = (active * up).astype(BF)
    hidden = join(hidden_h, core)
    back_out = move(dot(hidden, w_down, ((1,), (1,))).astype(BF))

    (hidden_grad,) = dp_sum([dot(grads, w_down, ((1,), (0,)))], core)
    d_up = join((hidden_grad * active).astype(BF), core)
    d_gate = join((hidden_grad * up * sigma * (1.0 + gate * (1.0 - sigma))).astype(BF), core)
    score = jnp.sum(hidden_grad * hidden_h.astype(F32), axis=1, keepdims=True)
    score = score + swap(score, "dp", 1)
    back_in = move((dot(d_gate, w_gate, ((1,), (1,))) + dot(d_up, w_up, ((1,), (1,)))).astype(BF))
    back_score = move(jnp.broadcast_to(score, (score.shape[0], 128)))[:, :1]

    grad_gate = dot(rows, d_gate, ((0,), (0,))).astype(BF)
    grad_up = dot(rows, d_up, ((0,), (0,))).astype(BF)
    grad_down = dot(grads, hidden, ((0,), (0,))).astype(BF)

    output = dot(pick_w, back_out, ((0,), (0,))).astype(BF)
    input_grad = dot(pick, back_in, ((0,), (0,))).astype(BF)

    per_token = jnp.sum(jnp.where(chosen, back_score.reshape(devices, CAP, 1), 0.0), axis=1)
    gate_grad = jnp.sum(
        jnp.where(match, per_token[:, None, :] / gate_values.T.astype(F32)[None], 0.0), axis=0
    ).T.astype(BF)
    return output, input_grad, gate_grad, grad_gate, grad_up, grad_down


def solution(mesh):
    in_specs = (
        P(("groups", "expert"), "dp"),
        P(("groups", "expert"), "dp"),
        P(("groups", "expert"), None),
        P(("groups", "expert"), None),
        P("dp", "expert"),
        P("dp", "expert"),
        P("dp", "expert"),
    )
    out_specs = (
        P(("groups", "expert"), "dp"),
        P(("groups", "expert"), "dp"),
        P(("groups", "expert"), None),
        P(("groups", "dp"), "expert"),
        P(("groups", "dp"), "expert"),
        P(("groups", "dp"), "expert"),
    )
    return jax.shard_map(
        per_device, mesh=mesh, in_specs=in_specs, out_specs=out_specs, check_vma=False
    )
```

time: 248 us -> 96.7 us (0.39)
  local copies, waits for them, and re-layouts: 68.2 us -> 1.59 us
  waiting for transfers between devices: 61.6 us -> 19.7 us
  other arithmetic: 26.2 us -> 4.09 us
  between operations: 14.2 us -> 0.95 us
  blocking collectives: 12.1 us -> 0 us
  starting transfers between devices: 20.6 us -> 29 us
  matrix products: 44.3 us -> 41 us
    gather x11 -> x0, local copies, waits for them, and re-layouts: 63.7 us -> none  [the longest x2 29.9 us: per_device(): picked_out = padded_out[labels[None, :], pick]]
    psum x1 -> x0, waiting for transfers between devices: 54.6 us -> none  [per_device(): gate, up = lax.psum((proj_gate, proj_up), 'dp')]
    ppermute x0 -> x25, starting transfers between devices: none -> 29 us  [swap(): return lax.ppermute(value, axis, [(i, i ^ step) for i in range(size)])]
    all_to_all x4 -> x0, starting transfers between devices: 20.5 us -> none  [the longest x1 6.45 us: per_device(): lax.all_to_all(jnp.repeat(pack_x, span, axis=0), 'expert', split_axis=0,...]
    ppermute x0 -> x25, waiting for transfers between devices: none -> 19.7 us  [swap(): return lax.ppermute(value, axis, [(i, i ^ step) for i in range(size)])]
    reduce_sum x5 -> x4, other arithmetic: 18.9 us -> 1.97 us  [the longest x1 0.78 us: per_device(): jnp.sum(jnp.where(match, gate_values.T.astype(F32)[None], 0.0), axis=1)]
    psum x1 -> x0, blocking collectives: 12.1 us -> none  [per_device(): lax.psum(jnp.sum(cotangent.astype(jnp.float32)[:, None, :] * picked_out,...]
    all_to_all x4 -> x0, waiting for transfers between devices: 6.92 us -> none  [the longest x1 5.58 us: per_device(): lax.all_to_all(jnp.repeat(pack_x, span, axis=0), 'expert', split_axis=0,...]
  transfers between devices with their start and end apart: 5 -> 25, of which waited for: 3 -> 7; matrix products, arithmetic and copies ran while one was open for 29% -> 44% of each run, Pallas kernels for 0% -> 0%
where the time goes in v1:
time: 96.7 us; the launch traced here: 96.4 us
  matrix products  41 us (42%)
  starting transfers between devices  29 us (30%)
  waiting for transfers between devices  19.7 us (20%)
  other arithmetic  4.09 us (4%)
  local copies, waits for them, and re-layouts  1.59 us (2%)
    dot_general x14, matrix products, dot(): lax.dot_general(left, right, (dims, ((), ())), preferred_element_type=F32)  41 us
    ppermute x25, starting transfers between devices, swap(): return lax.ppermute(value, axis, [(i, i ^ step) for i in range(size)])  29 us
    ppermute x25, waiting for transfers between devices, swap(): return lax.ppermute(value, axis, [(i, i ^ step) for i in range(size)])  19.7 us
  transfers between devices with their start and end apart: 25, of which 7 were waited for; matrix products, arithmetic and copies ran while one was open for 44% of the time, Pallas kernels for 0%

profile of v1, /device:TPU:0, one launch (start us, length us, event | category | flops | bytes accessed | tf_op | source)
XLA Modules:
  0.0 96.4 jit_solution(10646192118935523170)
XLA Ops:
  2.2 3.1 %collective-permute-start = (bf16[24,1792]{1,0:T(8,128)(2,1)S(1)}, bf16[24,1792]{1,0:T(8,128)(2,1)S(1)}, u32[]{:S(2)}, u32[]{:S(2)}) collective-permute-start(bf16[24,1792]{1,0:T(8,128)(2,1)S(1)} %get-tuple-element.33), channel_id=1, source_target_pairs={{0,4},{4,0},{8,12},{12,8},{1,5},{5,1},{9,13},{13,9},{2,6},{6,2},{1... | collective-permute-start | bytes 258056 | tf_op jit(solution)/shard_map/ppermute | solution.py:18
  5.3 2.6 %collective-permute-start.1 = (bf16[24,1792]{1,0:T(8,128)(2,1)S(1)}, bf16[24,1792]{1,0:T(8,128)(2,1)S(1)}, u32[]{:S(2)}, u32[]{:S(2)}) collective-permute-start(bf16[24,1792]{1,0:T(8,128)(2,1)S(1)} %get-tuple-element.32), channel_id=1, source_target_pairs={{0,8},{4,12},{8,0},{12,4},{1,9},{5,13},{9,1},{13,5},{2,10},{6,14},... | collective-permute-start | bytes 258056 | tf_op jit(solution)/shard_map/ppermute | solution.py:18
  9.5 1.5 %convolution_convert_fusion.5 = bf16[96,1792]{1,0:T(8,128)(2,1)S(1)} fusion(bf16[96,256]{1,0:T(8,128)(2,1)S(1)} %fusion.18, bf16[256,1792]{1,0:T(8,128)(2,1)} %param.8), kind=kOutput, calls=%fused_computation.6 | convolution fusion | flops 88252416 | bytes 1310720 | tf_op jit(solution)/shard_map/dot_general | solution.py:13
  11.9 3.5 %collective-permute-start.12 = (bf16[24,1792]{1,0:T(8,128)(2,1)S(1)}, bf16[24,1792]{1,0:T(8,128)(2,1)S(1)}, u32[]{:S(2)}, u32[]{:S(2)}) collective-permute-start(bf16[24,1792]{1,0:T(8,128)(2,1)S(1)} %get-tuple-element.36), channel_id=1, source_target_pairs={{0,8},{4,12},{8,0},{12,4},{1,9},{5,13},{9,1},{13,5},{2,10},{6,14},... | collective-permute-start | bytes 258056 | tf_op jit(solution)/shard_map/ppermute | solution.py:18
  15.5 4.5 %fusion.35 = f32[96,2048]{1,0:T(8,128)S(1)} fusion(bf16[1792,2048]{1,0:T(8,128)(2,1)} %param.11, bf16[24,1792]{1,0:T(8,128)(2,1)S(1)} %collective-permute-done.2, bf16[24,1792]{1,0:T(8,128)(2,1)S(1)} %collective-permute-done.1, bf16[24,1792]{1,0:T(8,128)(2,1)S(1)} %collective-permute-done, bf16[24,1792]{1,0:T(8,128)(2,1)S(1)} %get-tuple-element.30), kind=kOutput, calls=%fused_computation.88 | convolution fusion | flops 706019328 | bytes 8470528 | tf_op jit(solution)/shard_map/dot_general | solution.py:13
  24.2 1.6 %collective-permute-start.4 = (bf16[96,1024]{1,0:T(8,128)(2,1)S(1)}, bf16[96,1024]{1,0:T(8,128)(2,1)S(1)}, u32[]{:S(2)}, u32[]{:S(2)}) collective-permute-start(bf16[96,1024]{1,0:T(8,128)(2,1)S(1)} %get-tuple-element.10), channel_id=1, source_target_pairs={{0,2},{1,3},{2,0},{3,1},{4,6},{5,7},{6,4},{7,5},{8,10},{9,11},{10,... | collective-permute-start | bytes 589832 | tf_op jit(solution)/shard_map/ppermute | solution.py:18
  26.5 1.6 %collective-permute-start.15 = (bf16[96,1024]{1,0:T(8,128)(2,1)S(1)}, bf16[96,1024]{1,0:T(8,128)(2,1)S(1)}, u32[]{:S(2)}, u32[]{:S(2)}) collective-permute-start(bf16[96,1024]{1,0:T(8,128)(2,1)S(1)} %get-tuple-element.8), channel_id=1, source_target_pairs={{0,2},{1,3},{2,0},{3,1},{4,6},{5,7},{6,4},{7,5},{8,10},{9,11},{10,... | collective-permute-start | bytes 589832 | tf_op jit(solution)/shard_map/ppermute | solution.py:18
  28.1 3.9 %collective-permute-done.4 = bf16[96,1024]{1,0:T(8,128)(2,1)S(1)} collective-permute-done((bf16[96,1024]{1,0:T(8,128)(2,1)S(1)}, bf16[96,1024]{1,0:T(8,128)(2,1)S(1)}, u32[]{:S(2)}, u32[]{:S(2)}) %collective-permute-start.4) | collective-permute-done | bytes 196640 | tf_op jit(solution)/shard_map/ppermute | solution.py:18
  32.0 4.2 %collective-permute-done.6 = bf16[96,1024]{1,0:T(8,128)(2,1)S(1)} collective-permute-done((bf16[96,1024]{1,0:T(8,128)(2,1)S(1)}, bf16[96,1024]{1,0:T(8,128)(2,1)S(1)}, u32[]{:S(2)}, u32[]{:S(2)}) %collective-permute-start.6) | collective-permute-done | bytes 196640 | tf_op jit(solution)/shard_map/ppermute | solution.py:18
  36.2 3.8 %collective-permute-done.15 = bf16[96,1024]{1,0:T(8,128)(2,1)S(1)} collective-permute-done((bf16[96,1024]{1,0:T(8,128)(2,1)S(1)}, bf16[96,1024]{1,0:T(8,128)(2,1)S(1)}, u32[]{:S(2)}, u32[]{:S(2)}) %collective-permute-start.15) | collective-permute-done | bytes 196640 | tf_op jit(solution)/shard_map/ppermute | solution.py:18
  41.7 1.8 %collective-permute-start.22 = (f32[24,128]{0,1:T(8,128)S(1)}, f32[24,128]{0,1:T(8,128)S(1)}, u32[]{:S(2)}, u32[]{:S(2)}) collective-permute-start(f32[24,128]{0,1:T(8,128)S(1)} %broadcast_in_dim.74), channel_id=1, source_target_pairs={{0,4},{4,0},{8,12},{12,8},{1,5},{5,1},{9,13},{13,9},{2,6},{6,2},{1... | collective-permute-start | bytes 36872 | tf_op jit(solution)/shard_map/ppermute | solution.py:18
  43.5 2.1 %collective-permute-start.23 = (f32[24,128]{0,1:T(8,128)S(1)}, f32[24,128]{0,1:T(8,128)S(1)}, u32[]{:S(2)}, u32[]{:S(2)}) collective-permute-start(f32[24,128]{0,1:T(8,128)S(1)} %broadcast_in_dim.75), channel_id=1, source_target_pairs={{0,8},{4,12},{8,0},{12,4},{1,9},{5,13},{9,1},{13,5},{2,10},{6,14},... | collective-permute-start | bytes 36872 | tf_op jit(solution)/shard_map/ppermute | solution.py:18
  49.0 3.0 %collective-permute-done.24 = f32[24,128]{0,1:T(8,128)S(1)} collective-permute-done((f32[24,128]{0,1:T(8,128)S(1)}, f32[24,128]{0,1:T(8,128)S(1)}, u32[]{:S(2)}, u32[]{:S(2)}) %collective-permute-start.24) | collective-permute-done | bytes 12320 | tf_op jit(solution)/shard_map/ppermute | solution.py:18
  53.0 5.6 %fusion.17 = f32[96,1792]{1,0:T(8,128)S(1)} fusion(bf16[1792,2048]{1,0:T(8,128)(2,1)} %param.12, bf16[96,1024]{1,0:T(8,128)(2,1)S(1)} %get-tuple-element.19, bf16[96,1024]{1,0:T(8,128)(2,1)S(1)} %get-tuple-element.18), kind=kOutput, calls=%fused_computation.43 | convolution fusion | flops 705429504 | bytes 8421376 | tf_op jit(solution)/shard_map/dot_general | solution.py:13
  58.7 5.6 %fusion = bf16[96,1792]{1,0:T(8,128)(2,1)S(1)} fusion(f32[96,1792]{1,0:T(8,128)S(1)} %fusion.17, bf16[1792,2048]{1,0:T(8,128)(2,1)} %param.11, bf16[96,1024]{1,0:T(8,128)(2,1)S(1)} %get-tuple-element.17, bf16[96,1024]{1,0:T(8,128)(2,1)S(1)} %get-tuple-element.16), kind=kOutput, calls=%fused_computation.9 | convolution fusion | flops 705773568 | bytes 8765440 | tf_op jit(solution)/shard_map/dot_general | solution.py:13
  64.3 1.7 %collective-permute-start.18 = (bf16[24,1792]{1,0:T(8,128)(2,1)S(1)}, bf16[24,1792]{1,0:T(8,128)(2,1)S(1)}, u32[]{:S(2)}, u32[]{:S(2)}) collective-permute-start(bf16[24,1792]{1,0:T(8,128)(2,1)S(1)} %get-tuple-element.25), channel_id=1, source_target_pairs={{0,4},{4,0},{8,12},{12,8},{1,5},{5,1},{9,13},{13,9},{2,6},{6,2},{1... | collective-permute-start | bytes 258056 | tf_op jit(solution)/shard_map/ppermute | solution.py:18
  66.0 1.5 %collective-permute-start.19 = (bf16[24,1792]{1,0:T(8,128)(2,1)S(1)}, bf16[24,1792]{1,0:T(8,128)(2,1)S(1)}, u32[]{:S(2)}, u32[]{:S(2)}) collective-permute-start(bf16[24,1792]{1,0:T(8,128)(2,1)S(1)} %get-tuple-element.24), channel_id=1, source_target_pairs={{0,8},{4,12},{8,0},{12,4},{1,9},{5,13},{9,1},{13,5},{2,10},{6,14},... | collective-permute-start | bytes 258056 | tf_op jit(solution)/shard_map/ppermute | solution.py:18
  68.9 2.4 %convolution_convert_fusion.6 = bf16[96,1792]{1,0:T(8,128)(2,1)S(1)} fusion(bf16[1792,2048]{1,0:T(8,128)(2,1)S(1)} %bitcast.44, bf16[96,1024]{1,0:T(8,128)(2,1)S(1)} %get-tuple-element.21, bf16[96,1024]{1,0:T(8,128)(2,1)S(1)} %get-tuple-element.20), kind=kOutput, calls=%fused_computation.7 | convolution fusion | flops 705601536 | bytes 8077312 | tf_op jit(solution)/shard_map/dot_general | solution.py:13
  71.2 2.6 %collective-permute-start.10 = (bf16[24,1792]{1,0:T(8,128)(2,1)S(1)}, bf16[24,1792]{1,0:T(8,128)(2,1)S(1)}, u32[]{:S(2)}, u32[]{:S(2)}) collective-permute-start(bf16[24,1792]{1,0:T(8,128)(2,1)S(1)} %get-tuple-element.27), channel_id=1, source_target_pairs={{0,12},{4,8},{8,4},{12,0},{1,13},{5,9},{9,5},{13,1},{2,14},{6,10},... | collective-permute-start | bytes 258056 | tf_op jit(solution)/shard_map/ppermute | solution.py:18
  73.9 5.4 %convolution_convert_fusion = bf16[1792,2048]{1,0:T(8,128)(2,1)} fusion(bf16[96,1024]{1,0:T(8,128)(2,1)S(1)} %get-tuple-element.21, bf16[96,1024]{1,0:T(8,128)(2,1)S(1)} %get-tuple-element.20, bf16[24,1792]{1,0:T(8,128)(2,1)S(1)} %collective-permute-done.13, bf16[24,1792]{1,0:T(8,128)(2,1)S(1)} %collective-permute-done.12, ...), kind=kOutput, calls=%fused_computation | convolution fusion | flops 710475776 | bytes 8077312 | tf_op jit(solution)/shard_map/dot_general | solution.py:13
  79.2 5.1 %convolution_convert_fusion.1 = bf16[1792,2048]{1,0:T(8,128)(2,1)} fusion(bf16[96,1024]{1,0:T(8,128)(2,1)S(1)} %get-tuple-element.19, bf16[96,1024]{1,0:T(8,128)(2,1)S(1)} %get-tuple-element.18, bf16[24,1792]{1,0:T(8,128)(2,1)S(1)} %collective-permute-done.2, bf16[24,1792]{1,0:T(8,128)(2,1)S(1)} %collective-permute-done.1, ...), kind=kOutput, calls=%fused_computation.1 | convolution fusion | flops 710475776 | bytes 8077312 | tf_op jit(solution)/shard_map/dot_general | solution.py:13
  84.4 5.2 %convolution_convert_fusion.2 = bf16[1792,2048]{1,0:T(8,128)(2,1)} fusion(bf16[96,1024]{1,0:T(8,128)(2,1)S(1)} %get-tuple-element.17, bf16[96,1024]{1,0:T(8,128)(2,1)S(1)} %get-tuple-element.16, bf16[24,1792]{1,0:T(8,128)(2,1)S(1)} %collective-permute-done.2, bf16[24,1792]{1,0:T(8,128)(2,1)S(1)} %collective-permute-done.1, ...), kind=kOutput, calls=%fused_computation.2 | convolution fusion | flops 710475776 | bytes 8077312 | tf_op jit(solution)/shard_map/dot_general | solution.py:13
  89.5 1.8 %collective-permute-start.9 = (bf16[24,1792]{1,0:T(8,128)(2,1)S(1)}, bf16[24,1792]{1,0:T(8,128)(2,1)S(1)}, u32[]{:S(2)}, u32[]{:S(2)}) collective-permute-start(bf16[24,1792]{1,0:T(8,128)(2,1)S(1)} %get-tuple-element.28), channel_id=1, source_target_pairs={{0,8},{4,12},{8,0},{12,4},{1,9},{5,13},{9,1},{13,5},{2,10},{6,14},... | collective-permute-start | bytes 258056 | tf_op jit(solution)/shard_map/ppermute | solution.py:18
  92.7 2.4 %collective-permute-done.9 = bf16[24,1792]{1,0:T(8,128)(2,1)S(1)} collective-permute-done((bf16[24,1792]{1,0:T(8,128)(2,1)S(1)}, bf16[24,1792]{1,0:T(8,128)(2,1)S(1)}, u32[]{:S(2)}, u32[]{:S(2)}) %collective-permute-start.9) | collective-permute-done | bytes 86048 | tf_op jit(solution)/shard_map/ppermute | solution.py:18
  (85 shorter events, 19.2 us)
Async XLA Ops:
  2.2 13.2 %collective-permute-start = (bf16[24,1792]{1,0:T(8,128)(2,1)S(1)}, bf16[24,1792]{1,0:T(8,128)(2,1)S(1)}, u32[]{:S(2)}, u32[]{:S(2)}) collective-permute-start(bf16[24,1792]{1,0:T(8,128)(2,1)S(1)} %get-tuple-element.33), channel_id=1, source_target_pairs={{0,4},{4,0},{8,12},{12,8},{1,5},{5,1},{9,13},{13,9},{2,6},{6,2},{1... | collective-permute-start | bytes 258056 | tf_op jit(solution)/shard_map/ppermute | solution.py:18
  5.3 10.1 %collective-permute-start.1 = (bf16[24,1792]{1,0:T(8,128)(2,1)S(1)}, bf16[24,1792]{1,0:T(8,128)(2,1)S(1)}, u32[]{:S(2)}, u32[]{:S(2)}) collective-permute-start(bf16[24,1792]{1,0:T(8,128)(2,1)S(1)} %get-tuple-element.32), channel_id=1, source_target_pairs={{0,8},{4,12},{8,0},{12,4},{1,9},{5,13},{9,1},{13,5},{2,10},{6,14},... | collective-permute-start | bytes 258056 | tf_op jit(solution)/shard_map/ppermute | solution.py:18
  7.9 7.6 %collective-permute-start.2 = (bf16[24,1792]{1,0:T(8,128)(2,1)S(1)}, bf16[24,1792]{1,0:T(8,128)(2,1)S(1)}, u32[]{:S(2)}, u32[]{:S(2)}) collective-permute-start(bf16[24,1792]{1,0:T(8,128)(2,1)S(1)} %get-tuple-element.31), channel_id=1, source_target_pairs={{0,12},{4,8},{8,4},{12,0},{1,13},{5,9},{9,5},{13,1},{2,14},{6,10},... | collective-permute-start | bytes 258056 | tf_op jit(solution)/shard_map/ppermute | solution.py:18
  11.0 11.1 %collective-permute-start.11 = (bf16[24,1792]{1,0:T(8,128)(2,1)S(1)}, bf16[24,1792]{1,0:T(8,128)(2,1)S(1)}, u32[]{:S(2)}, u32[]{:S(2)}) collective-permute-start(bf16[24,1792]{1,0:T(8,128)(2,1)S(1)} %get-tuple-element.37), channel_id=1, source_target_pairs={{0,4},{4,0},{8,12},{12,8},{1,5},{5,1},{9,13},{13,9},{2,6},{6,2},{1... | collective-permute-start | bytes 258056 | tf_op jit(solution)/shard_map/ppermute | solution.py:18
  11.9 10.1 %collective-permute-start.12 = (bf16[24,1792]{1,0:T(8,128)(2,1)S(1)}, bf16[24,1792]{1,0:T(8,128)(2,1)S(1)}, u32[]{:S(2)}, u32[]{:S(2)}) collective-permute-start(bf16[24,1792]{1,0:T(8,128)(2,1)S(1)} %get-tuple-element.36), channel_id=1, source_target_pairs={{0,8},{4,12},{8,0},{12,4},{1,9},{5,13},{9,1},{13,5},{2,10},{6,14},... | collective-permute-start | bytes 258056 | tf_op jit(solution)/shard_map/ppermute | solution.py:18
  15.4 6.6 %collective-permute-start.13 = (bf16[24,1792]{1,0:T(8,128)(2,1)S(1)}, bf16[24,1792]{1,0:T(8,128)(2,1)S(1)}, u32[]{:S(2)}, u32[]{:S(2)}) collective-permute-start(bf16[24,1792]{1,0:T(8,128)(2,1)S(1)} %get-tuple-element.35), channel_id=1, source_target_pairs={{0,12},{4,8},{8,4},{12,0},{1,13},{5,9},{9,5},{13,1},{2,14},{6,10},... | collective-permute-start | bytes 258056 | tf_op jit(solution)/shard_map/ppermute | solution.py:18
  20.1 4.1 %collective-permute-start.3 = (f32[96,1024]{1,0:T(8,128)S(1)}, f32[96,1024]{1,0:T(8,128)S(1)}, u32[]{:S(2)}, u32[]{:S(2)}) collective-permute-start(f32[96,1024]{1,0:T(8,128)S(1)} %constant_dynamic-slice_fusion.2), channel_id=1, source_target_pairs={{0,1},{1,0},{2,3},{3,2},{4,5},{5,4},{6,7},{7,6},{8,9},{9,8},{10,11... | collective-permute-start | bytes 1179656 | tf_op jit(solution)/shard_map/ppermute | solution.py:18
  22.0 3.9 %collective-permute-start.5 = (f32[96,1024]{1,0:T(8,128)S(1)}, f32[96,1024]{1,0:T(8,128)S(1)}, u32[]{:S(2)}, u32[]{:S(2)}) collective-permute-start(f32[96,1024]{1,0:T(8,128)S(1)} %constant_dynamic-slice_fusion.1), channel_id=1, source_target_pairs={{0,1},{1,0},{2,3},{3,2},{4,5},{5,4},{6,7},{7,6},{8,9},{9,8},{10,11... | collective-permute-start | bytes 1179656 | tf_op jit(solution)/shard_map/ppermute | solution.py:18
  24.1 2.4 %collective-permute-start.14 = (f32[96,1024]{1,0:T(8,128)S(1)}, f32[96,1024]{1,0:T(8,128)S(1)}, u32[]{:S(2)}, u32[]{:S(2)}) collective-permute-start(f32[96,1024]{1,0:T(8,128)S(1)} %constant_dynamic-slice_fusion), channel_id=1, source_target_pairs={{0,1},{1,0},{2,3},{3,2},{4,5},{5,4},{6,7},{7,6},{8,9},{9,8},{10,11... | collective-permute-start | bytes 1179656 | tf_op jit(solution)/shard_map/ppermute | solution.py:18
  24.2 7.8 %collective-permute-start.4 = (bf16[96,1024]{1,0:T(8,128)(2,1)S(1)}, bf16[96,1024]{1,0:T(8,128)(2,1)S(1)}, u32[]{:S(2)}, u32[]{:S(2)}) collective-permute-start(bf16[96,1024]{1,0:T(8,128)(2,1)S(1)} %get-tuple-element.10), channel_id=1, source_target_pairs={{0,2},{1,3},{2,0},{3,1},{4,6},{5,7},{6,4},{7,5},{8,10},{9,11},{10,... | collective-permute-start | bytes 589832 | tf_op jit(solution)/shard_map/ppermute | solution.py:18
  25.9 10.3 %collective-permute-start.6 = (bf16[96,1024]{1,0:T(8,128)(2,1)S(1)}, bf16[96,1024]{1,0:T(8,128)(2,1)S(1)}, u32[]{:S(2)}, u32[]{:S(2)}) collective-permute-start(bf16[96,1024]{1,0:T(8,128)(2,1)S(1)} %get-tuple-element.12), channel_id=1, source_target_pairs={{0,2},{1,3},{2,0},{3,1},{4,6},{5,7},{6,4},{7,5},{8,10},{9,11},{10,... | collective-permute-start | bytes 589832 | tf_op jit(solution)/shard_map/ppermute | solution.py:18
  26.5 13.5 %collective-permute-start.15 = (bf16[96,1024]{1,0:T(8,128)(2,1)S(1)}, bf16[96,1024]{1,0:T(8,128)(2,1)S(1)}, u32[]{:S(2)}, u32[]{:S(2)}) collective-permute-start(bf16[96,1024]{1,0:T(8,128)(2,1)S(1)} %get-tuple-element.8), channel_id=1, source_target_pairs={{0,2},{1,3},{2,0},{3,1},{4,6},{5,7},{6,4},{7,5},{8,10},{9,11},{10,... | collective-permute-start | bytes 589832 | tf_op jit(solution)/shard_map/ppermute | solution.py:18
  41.7 5.9 %collective-permute-start.22 = (f32[24,128]{0,1:T(8,128)S(1)}, f32[24,128]{0,1:T(8,128)S(1)}, u32[]{:S(2)}, u32[]{:S(2)}) collective-permute-start(f32[24,128]{0,1:T(8,128)S(1)} %broadcast_in_dim.74), channel_id=1, source_target_pairs={{0,4},{4,0},{8,12},{12,8},{1,5},{5,1},{9,13},{13,9},{2,6},{6,2},{1... | collective-permute-start | bytes 36872 | tf_op jit(solution)/shard_map/ppermute | solution.py:18
  43.5 5.5 %collective-permute-start.23 = (f32[24,128]{0,1:T(8,128)S(1)}, f32[24,128]{0,1:T(8,128)S(1)}, u32[]{:S(2)}, u32[]{:S(2)}) collective-permute-start(f32[24,128]{0,1:T(8,128)S(1)} %broadcast_in_dim.75), channel_id=1, source_target_pairs={{0,8},{4,12},{8,0},{12,4},{1,9},{5,13},{9,1},{13,5},{2,10},{6,14},... | collective-permute-start | bytes 36872 | tf_op jit(solution)/shard_map/ppermute | solution.py:18
  45.6 6.4 %collective-permute-start.24 = (f32[24,128]{0,1:T(8,128)S(1)}, f32[24,128]{0,1:T(8,128)S(1)}, u32[]{:S(2)}, u32[]{:S(2)}) collective-permute-start(f32[24,128]{0,1:T(8,128)S(1)} %broadcast_in_dim.76), channel_id=1, source_target_pairs={{0,12},{4,8},{8,4},{12,0},{1,13},{5,9},{9,5},{13,1},{2,14},{6,10},... | collective-permute-start | bytes 36872 | tf_op jit(solution)/shard_map/ppermute | solution.py:18
  47.0 21.8 %collective-permute-start.7 = (bf16[96,1024]{1,0:T(8,128)(2,1)S(1)}, bf16[96,1024]{1,0:T(8,128)(2,1)S(1)}, u32[]{:S(2)}, u32[]{:S(2)}) collective-permute-start(bf16[96,1024]{1,0:T(8,128)(2,1)S(1)} %get-tuple-element.7), channel_id=1, source_target_pairs={{0,1},{1,0},{2,3},{3,2},{4,5},{5,4},{6,7},{7,6},{8,9},{9,8},{10,11... | collective-permute-start | bytes 589832 | tf_op jit(solution)/shard_map/ppermute | solution.py:18
  47.0 5.9 %collective-permute-start.17 = (bf16[96,1024]{1,0:T(8,128)(2,1)S(1)}, bf16[96,1024]{1,0:T(8,128)(2,1)S(1)}, u32[]{:S(2)}, u32[]{:S(2)}) collective-permute-start(bf16[96,1024]{1,0:T(8,128)(2,1)S(1)} %get-tuple-element.15), channel_id=1, source_target_pairs={{0,1},{1,0},{2,3},{3,2},{4,5},{5,4},{6,7},{7,6},{8,9},{9,8},{10,11... | collective-permute-start | bytes 589832 | tf_op jit(solution)/shard_map/ppermute | solution.py:18
  47.6 11.1 %collective-permute-start.16 = (bf16[96,1024]{1,0:T(8,128)(2,1)S(1)}, bf16[96,1024]{1,0:T(8,128)(2,1)S(1)}, u32[]{:S(2)}, u32[]{:S(2)}) collective-permute-start(bf16[96,1024]{1,0:T(8,128)(2,1)S(1)} %get-tuple-element.14), channel_id=1, source_target_pairs={{0,1},{1,0},{2,3},{3,2},{4,5},{5,4},{6,7},{7,6},{8,9},{9,8},{10,11... | collective-permute-start | bytes 589832 | tf_op jit(solution)/shard_map/ppermute | solution.py:18
  64.3 25.2 %collective-permute-start.18 = (bf16[24,1792]{1,0:T(8,128)(2,1)S(1)}, bf16[24,1792]{1,0:T(8,128)(2,1)S(1)}, u32[]{:S(2)}, u32[]{:S(2)}) collective-permute-start(bf16[24,1792]{1,0:T(8,128)(2,1)S(1)} %get-tuple-element.25), channel_id=1, source_target_pairs={{0,4},{4,0},{8,12},{12,8},{1,5},{5,1},{9,13},{13,9},{2,6},{6,2},{1... | collective-permute-start | bytes 258056 | tf_op jit(solution)/shard_map/ppermute | solution.py:18
  66.0 25.4 %collective-permute-start.19 = (bf16[24,1792]{1,0:T(8,128)(2,1)S(1)}, bf16[24,1792]{1,0:T(8,128)(2,1)S(1)}, u32[]{:S(2)}, u32[]{:S(2)}) collective-permute-start(bf16[24,1792]{1,0:T(8,128)(2,1)S(1)} %get-tuple-element.24), channel_id=1, source_target_pairs={{0,8},{4,12},{8,0},{12,4},{1,9},{5,13},{9,1},{13,5},{2,10},{6,14},... | collective-permute-start | bytes 258056 | tf_op jit(solution)/shard_map/ppermute | solution.py:18
  67.5 23.9 %collective-permute-start.20 = (bf16[24,1792]{1,0:T(8,128)(2,1)S(1)}, bf16[24,1792]{1,0:T(8,128)(2,1)S(1)}, u32[]{:S(2)}, u32[]{:S(2)}) collective-permute-start(bf16[24,1792]{1,0:T(8,128)(2,1)S(1)} %get-tuple-element.23), channel_id=1, source_target_pairs={{0,12},{4,8},{8,4},{12,0},{1,13},{5,9},{9,5},{13,1},{2,14},{6,10},... | collective-permute-start | bytes 258056 | tf_op jit(solution)/shard_map/ppermute | solution.py:18
  71.2 21.5 %collective-permute-start.10 = (bf16[24,1792]{1,0:T(8,128)(2,1)S(1)}, bf16[24,1792]{1,0:T(8,128)(2,1)S(1)}, u32[]{:S(2)}, u32[]{:S(2)}) collective-permute-start(bf16[24,1792]{1,0:T(8,128)(2,1)S(1)} %get-tuple-element.27), channel_id=1, source_target_pairs={{0,12},{4,8},{8,4},{12,0},{1,13},{5,9},{9,5},{13,1},{2,14},{6,10},... | collective-permute-start | bytes 258056 | tf_op jit(solution)/shard_map/ppermute | solution.py:18
  73.8 18.9 %collective-permute-start.8 = (bf16[24,1792]{1,0:T(8,128)(2,1)S(1)}, bf16[24,1792]{1,0:T(8,128)(2,1)S(1)}, u32[]{:S(2)}, u32[]{:S(2)}) collective-permute-start(bf16[24,1792]{1,0:T(8,128)(2,1)S(1)} %get-tuple-element.29), channel_id=1, source_target_pairs={{0,4},{4,0},{8,12},{12,8},{1,5},{5,1},{9,13},{13,9},{2,6},{6,2},{1... | collective-permute-start | bytes 258056 | tf_op jit(solution)/shard_map/ppermute | solution.py:18
  89.5 5.6 %collective-permute-start.9 = (bf16[24,1792]{1,0:T(8,128)(2,1)S(1)}, bf16[24,1792]{1,0:T(8,128)(2,1)S(1)}, u32[]{:S(2)}, u32[]{:S(2)}) collective-permute-start(bf16[24,1792]{1,0:T(8,128)(2,1)S(1)} %get-tuple-element.28), channel_id=1, source_target_pairs={{0,8},{4,12},{8,0},{12,4},{1,9},{5,13},{9,1},{13,5},{2,10},{6,14},... | collective-permute-start | bytes 258056 | tf_op jit(solution)/shard_map/ppermute | solution.py:18
  (7 other events, 70.4 us)

commit v2 on v1

v2 whole, which is shorter than its diff:
```python
import jax
import jax.numpy as jnp
from jax import lax
from jax.experimental import pallas as pl
from jax.experimental.pallas import tpu as pltpu
from jax.sharding import PartitionSpec as P

EXPERTS = 4
CAP = 24
EXTRA = 128
BF = jnp.bfloat16
F32 = jnp.float32


def dot(left, right, dims):
    return lax.dot_general(left, right, (dims, ((), ())), preferred_element_type=F32)


def swap(value, axis, step):
    size = lax.axis_size(axis)
    return lax.ppermute(value, axis, [(i, i ^ step) for i in range(size)])


def exchange(blocks, axis):
    return [blocks[0]] + [swap(blocks[s], axis, s) for s in range(1, len(blocks))]


def dp_sum(values, even):
    size = lax.axis_size("dp")
    half = values[0].shape[1] // 2
    mine = [jnp.where(even, v[:, :half], v[:, half:]) for v in values]
    other = [jnp.where(even, v[:, half:], v[:, :half]) for v in values]
    got = swap(jnp.concatenate(other, axis=1), "dp", 1)
    total = jnp.concatenate(mine, axis=1) + got
    step = 2
    while step < size:
        total = total + swap(total.astype(BF), "dp", step).astype(F32)
        step *= 2
    return [total[:, i * half:(i + 1) * half] for i in range(len(values))]


def join(values, even):
    half = values[0].shape[1]
    other = swap(jnp.concatenate(values, axis=1), "dp", 1)
    out = []
    for i, v in enumerate(values):
        o = other[:, i * half:(i + 1) * half]
        out.append(jnp.concatenate([jnp.where(even, v, o), jnp.where(even, o, v)], axis=1))
    return out


def weight_grads(rows, cots):
    count, width = rows.shape
    hidden = cots[0].shape[1]
    n = len(cots)
    block = width // 7 if width % (7 * 128) == 0 else 128

    def body(rows_ref, *refs):
        cot_refs, outs, buf, sem = refs[:n], refs[n:2 * n], refs[2 * n], refs[2 * n + 1]
        values = [c[...] for c in cot_refs]
        for at in range(0, width, block):
            part = rows_ref[:, at:at + block]
            for i in range(n):
                buf[i, at:at + block, :] = dot(part, values[i], ((0,), (0,))).astype(BF)
                pltpu.make_async_copy(
                    buf.at[i, pl.ds(at, block)], outs[i].at[pl.ds(at, block)], sem.at[i]
                ).start()
        for i in range(n):
            pltpu.make_async_copy(buf.at[i], outs[i], sem.at[i]).wait()

    size = n * width * hidden * 2
    vmem = pl.BlockSpec(memory_space=pltpu.VMEM)
    return pl.pallas_call(
        body,
        in_specs=[vmem] * (n + 1),
        out_specs=[pl.BlockSpec(memory_space=pl.ANY)] * n,
        out_shape=[jax.ShapeDtypeStruct((width, hidden), BF)] * n,
        scratch_shapes=[pltpu.VMEM((n, width, hidden), BF), pltpu.SemaphoreType.DMA((n,))],
        compiler_params=pltpu.CompilerParams(vmem_limit_bytes=size + (8 << 20)),
        cost_estimate=pl.CostEstimate(flops=size * count, bytes_accessed=size, transcendentals=0),
    )(rows, *cots)


def per_device(tokens, cotangent, expert_ids, gate_values, w_gate, w_up, w_down):
    devices = lax.axis_size("expert")
    span = devices // EXPERTS
    count, width = tokens.shape
    direct = devices <= 8
    even = lax.axis_index("dp") % 2 == 0
    me = lax.axis_index("expert")
    expert_ids, even, me = lax.optimization_barrier((expert_ids, even, me))

    steps = jnp.arange(devices, dtype=jnp.int32)
    labels = ((steps ^ me) if direct else steps) // span
    match = expert_ids.T[None, :, :] == labels[:, None, None]
    member = jnp.any(match, axis=1)
    weight = jnp.sum(jnp.where(match, gate_values.T.astype(F32)[None], 0.0), axis=1)
    earlier = jnp.arange(count)[:, None] < jnp.arange(count)[None, :]
    slot = dot(member.astype(BF), earlier.astype(BF), ((1,), (0,)))
    places = jnp.arange(CAP, dtype=F32)
    chosen = (slot[:, None, :] == places[None, :, None]) & member[:, None, :]
    pick = chosen.astype(BF).reshape(devices * CAP, count)
    pick_w = jnp.where(chosen, weight[:, None, :], 0.0).astype(BF).reshape(devices * CAP, count)

    def move(rows):
        if direct:
            return jnp.concatenate(
                exchange([rows[s * CAP:(s + 1) * CAP] for s in range(devices)], "expert"), axis=0)
        got = lax.all_to_all(rows.reshape(devices, CAP, -1), "expert", split_axis=0, concat_axis=0, tiled=True)
        return got.reshape(devices * CAP, -1)

    rows = move(dot(pick, tokens, ((1,), (0,))).astype(BF))
    grads = move(dot(pick_w, cotangent, ((1,), (0,))).astype(BF))

    gate, up = dp_sum([dot(rows, w_gate, ((1,), (0,))), dot(rows, w_up, ((1,), (0,)))], even)
    sigma = jax.nn.sigmoid(gate)
    active = gate * sigma
    hidden_h = (active * up).astype(BF)
    (hidden,) = join([hidden_h], even)
    back_out = move(dot(hidden, w_down, ((1,), (1,))).astype(BF))

    (hidden_grad,) = dp_sum([dot(grads, w_down, ((1,), (0,)))], even)
    d_up, d_gate = join(
        [
            (hidden_grad * active).astype(BF),
            (hidden_grad * up * sigma * (1.0 + gate * (1.0 - sigma))).astype(BF),
        ],
        even,
    )
    score = jnp.sum(hidden_grad * hidden_h.astype(F32), axis=1, keepdims=True)
    score = score + swap(score, "dp", 1)
    high = lax.reduce_precision(score, 8, 7)
    low = (score - high).astype(BF)
    high = high.astype(BF)
    lanes = jnp.arange(EXTRA)[None, :]
    extra = jnp.where(lanes < EXTRA // 2, high, low)
    part_in = (dot(d_gate, w_gate, ((1,), (1,))) + dot(d_up, w_up, ((1,), (1,)))).astype(BF)
    back_in = move(jnp.concatenate([part_in, extra], axis=1))

    late_grads, late_w = lax.optimization_barrier((grads, pick_w, part_in))[:2]
    (grad_down,) = weight_grads(late_grads, [hidden])
    grad_gate, grad_up = weight_grads(rows, [d_gate, d_up])

    output = dot(late_w, back_out, ((0,), (0,))).astype(BF)
    input_grad = dot(pick, back_in[:, :width], ((0,), (0,))).astype(BF)

    source = jnp.arange(devices * CAP)[:, None] // CAP
    placed = jnp.where(source == lanes % (EXTRA // 2), back_in[:, width:], jnp.zeros((), BF))
    per_token = dot(placed, pick, ((0,), (0,)))
    per_token = per_token[:devices] + per_token[EXTRA // 2:EXTRA // 2 + devices]
    gate_grad = jnp.sum(
        jnp.where(match, per_token[:, None, :] / gate_values.T.astype(F32)[None], 0.0), axis=0
    ).T.astype(BF)
    return output, input_grad, gate_grad, grad_gate, grad_up, grad_down


def solution(mesh):
    in_specs = (
        P(("groups", "expert"), "dp"),
        P(("groups", "expert"), "dp"),
        P(("groups", "expert"), None),
        P(("groups", "expert"), None),
        P("dp", "expert"),
        P("dp", "expert"),
        P("dp", "expert"),
    )
    out_specs = (
        P(("groups", "expert"), "dp"),
        P(("groups", "expert"), "dp"),
        P(("groups", "expert"), None),
        P(("groups", "dp"), "expert"),
        P(("groups", "dp"), "expert"),
        P(("groups", "dp"), "expert"),
    )
    return jax.shard_map(
        per_device, mesh=mesh, in_specs=in_specs, out_specs=out_specs, check_vma=False
    )
```

time: 96.7 us -> 72.7 us (0.75)
  matrix products: 41 us -> 19.2 us
  Pallas kernels: 0 us -> 9.26 us
  waiting for transfers between devices: 19.7 us -> 13.6 us
  starting transfers between devices: 29 us -> 24.4 us
  local copies, waits for them, and re-layouts: 1.59 us -> 0.31 us
    dot_general x14 -> x12, matrix products: 41 us -> 19.2 us  [dot(): lax.dot_general(left, right, (dims, ((), ())), preferred_element_type=F32)]
    pallas_call x0 -> x2, Pallas kernels: none -> 9.26 us  [weight_grads(): pl.pallas_call(body, in_specs=[vmem] * (n + 1), out_specs=[pl.BlockSpec(m...]
    ppermute x25 -> x19, waiting for transfers between devices: 19.7 us -> 13.6 us  [swap(): return lax.ppermute(value, axis, [(i, i ^ step) for i in range(size)])]
    ppermute x25 -> x19, starting transfers between devices: 29 us -> 24.4 us  [swap(): return lax.ppermute(value, axis, [(i, i ^ step) for i in range(size)])]
  transfers between devices with their start and end apart: 25 -> 19, of which waited for: 7 -> 5; matrix products, arithmetic and copies ran while one was open for 44% -> 27% of each run, Pallas kernels for 0% -> 13%
where the time goes in v2:
time: 72.7 us; the launch traced here: 72.4 us
  starting transfers between devices  24.4 us (34%)
  matrix products  19.2 us (26%)
  waiting for transfers between devices  13.6 us (19%)
  Pallas kernels  9.26 us (13%)
  other arithmetic  4.58 us (6%)
  between operations  1.06 us (1%)
    ppermute x19, starting transfers between devices, swap(): return lax.ppermute(value, axis, [(i, i ^ step) for i in range(size)])  24.4 us
    dot_general x12, matrix products, dot(): lax.dot_general(left, right, (dims, ((), ())), preferred_element_type=F32)  19.2 us
    ppermute x19, waiting for transfers between devices, swap(): return lax.ppermute(value, axis, [(i, i ^ step) for i in range(size)])  13.6 us
    pallas_call x2, Pallas kernels, weight_grads(): pl.pallas_call(body, in_specs=[vmem] * (n + 1), out_specs=[pl.BlockSpec(m...  9.26 us
  transfers between devices with their start and end apart: 19, of which 5 were waited for; matrix products, arithmetic and copies ran while one was open for 27% of the time, Pallas kernels for 13%

profile of v2, /device:TPU:0, one launch (start us, length us, event | category | flops | bytes accessed | tf_op | source)
XLA Modules:
  0.0 72.4 jit_solution(5084574445436569745)
XLA Ops:
  2.2 3.1 %collective-permute-start.5 = (bf16[24,1792]{1,0:T(8,128)(2,1)S(1)}, bf16[24,1792]{1,0:T(8,128)(2,1)S(1)}, u32[]{:S(2)}, u32[]{:S(2)}) collective-permute-start(bf16[24,1792]{1,0:T(8,128)(2,1)S(1)} %get-tuple-element.49), channel_id=1, source_target_pairs={{0,4},{4,0},{8,12},{12,8},{1,5},{5,1},{9,13},{13,9},{2,6},{6,2},{1... | collective-permute-start | bytes 258056 | tf_op jit(solution)/shard_map/ppermute | solution.py:21
  5.3 2.6 %collective-permute-start.6 = (bf16[24,1792]{1,0:T(8,128)(2,1)S(1)}, bf16[24,1792]{1,0:T(8,128)(2,1)S(1)}, u32[]{:S(2)}, u32[]{:S(2)}) collective-permute-start(bf16[24,1792]{1,0:T(8,128)(2,1)S(1)} %get-tuple-element.48), channel_id=1, source_target_pairs={{0,8},{4,12},{8,0},{12,4},{1,9},{5,13},{9,1},{13,5},{2,10},{6,14},... | collective-permute-start | bytes 258056 | tf_op jit(solution)/shard_map/ppermute | solution.py:21
  9.5 1.5 %convolution_convert_fusion.4 = bf16[96,1792]{1,0:T(8,128)(2,1)S(1)} fusion(bf16[96,256]{1,0:T(8,128)(2,1)S(1)} %fusion.12, bf16[256,1792]{1,0:T(8,128)(2,1)} %param.8), kind=kOutput, calls=%fused_computation.5 | convolution fusion | flops 88252416 | bytes 1310720 | tf_op jit(solution)/shard_map/dot_general | solution.py:16
  11.0 1.0 %collective-permute-start = (bf16[24,1792]{1,0:T(8,128)(2,1)S(1)}, bf16[24,1792]{1,0:T(8,128)(2,1)S(1)}, u32[]{:S(2)}, u32[]{:S(2)}) collective-permute-start(bf16[24,1792]{1,0:T(8,128)(2,1)S(1)} %get-tuple-element.53), channel_id=1, source_target_pairs={{0,4},{4,0},{8,12},{12,8},{1,5},{5,1},{9,13},{13,9},{2,6},{6,2},{1... | collective-permute-start | bytes 258056 | tf_op jit(solution)/shard_map/ppermute | solution.py:21
  11.9 3.5 %collective-permute-start.1 = (bf16[24,1792]{1,0:T(8,128)(2,1)S(1)}, bf16[24,1792]{1,0:T(8,128)(2,1)S(1)}, u32[]{:S(2)}, u32[]{:S(2)}) collective-permute-start(bf16[24,1792]{1,0:T(8,128)(2,1)S(1)} %get-tuple-element.52), channel_id=1, source_target_pairs={{0,8},{4,12},{8,0},{12,4},{1,9},{5,13},{9,1},{13,5},{2,10},{6,14},... | collective-permute-start | bytes 258056 | tf_op jit(solution)/shard_map/ppermute | solution.py:21
  15.6 4.6 %fusion.38 = f32[96,2048]{1,0:T(8,128)S(1)} fusion(bf16[1792,2048]{1,0:T(8,128)(2,1)} %param.12, bf16[24,1792]{1,0:T(8,128)(2,1)S(1)} %collective-permute-done.7, bf16[24,1792]{1,0:T(8,128)(2,1)S(1)} %collective-permute-done.6, bf16[24,1792]{1,0:T(8,128)(2,1)S(1)} %collective-permute-done.5, bf16[24,1792]{1,0:T(8,128)(2,1)S(1)} %get-tuple-element.46), kind=kOutput, calls=%fused_computation.99 | convolution fusion | flops 706019328 | bytes 8470528 | tf_op jit(solution)/shard_map/dot_general | solution.py:16
  20.1 1.3 %fusion.39 = f32[96,2048]{1,0:T(8,128)S(1)} fusion(bf16[1792,2048]{1,0:T(8,128)(2,1)S(1)} %copy-done.1, bf16[24,1792]{1,0:T(8,128)(2,1)S(1)} %collective-permute-done.7, bf16[24,1792]{1,0:T(8,128)(2,1)S(1)} %collective-permute-done.6, bf16[24,1792]{1,0:T(8,128)(2,1)S(1)} %collective-permute-done.5, bf16[24,1792]{1,0:T(8,128)(2,1)S(1)} %get-tuple-element.46), kind=kOutput, calls=%fused_computation.100 | convolution fusion | flops 706019328 | bytes 8470528 | tf_op jit(solution)/shard_map/dot_general | solution.py:16
  22.0 1.3 %fusion.37 = f32[96,2048]{1,0:T(8,128)S(1)} fusion(bf16[1792,2048]{1,0:T(8,128)(2,1)S(1)} %bitcast.42, bf16[24,1792]{1,0:T(8,128)(2,1)S(1)} %collective-permute-done.2, bf16[24,1792]{1,0:T(8,128)(2,1)S(1)} %collective-permute-done.1, bf16[24,1792]{1,0:T(8,128)(2,1)S(1)} %collective-permute-done, bf16[24,1792]{1,0:T(8,128)(2,1)S(1)} %get-tuple-element.50), kind=kOutput, calls=%fused_computation.98 | convolution fusion | flops 706019328 | bytes 8470528 | tf_op jit(solution)/shard_map/dot_general | solution.py:16
  24.2 1.7 %collective-permute-start.9 = (bf16[96,2048]{1,0:T(8,128)(2,1)S(1)}, bf16[96,2048]{1,0:T(8,128)(2,1)S(1)}, u32[]{:S(2)}, u32[]{:S(2)}) collective-permute-start(bf16[96,2048]{1,0:T(8,128)(2,1)S(1)} %fusion.11), channel_id=1, source_target_pairs={{0,2},{1,3},{2,0},{3,1},{4,6},{5,7},{6,4},{7,5},{8,10},{9,11},{10,... | collective-permute-start | bytes 1179656 | tf_op jit(solution)/shard_map/ppermute | solution.py:21
  26.0 1.0 %collective-permute-start.4 = (bf16[96,1024]{1,0:T(8,128)(2,1)S(1)}, bf16[96,1024]{1,0:T(8,128)(2,1)S(1)}, u32[]{:S(2)}, u32[]{:S(2)}) collective-permute-start(bf16[96,1024]{1,0:T(8,128)(2,1)S(1)} %get-tuple-element.22), channel_id=1, source_target_pairs={{0,2},{1,3},{2,0},{3,1},{4,6},{5,7},{6,4},{7,5},{8,10},{9,11},{10,... | collective-permute-start | bytes 589832 | tf_op jit(solution)/shard_map/ppermute | solution.py:21
  27.0 9.2 %collective-permute-done.9 = bf16[96,2048]{1,0:T(8,128)(2,1)S(1)} collective-permute-done((bf16[96,2048]{1,0:T(8,128)(2,1)S(1)}, bf16[96,2048]{1,0:T(8,128)(2,1)S(1)}, u32[]{:S(2)}, u32[]{:S(2)}) %collective-permute-start.9) | collective-permute-done | bytes 393248 | tf_op jit(solution)/shard_map/ppermute | solution.py:21
  36.3 3.3 %collective-permute-done.4 = bf16[96,1024]{1,0:T(8,128)(2,1)S(1)} collective-permute-done((bf16[96,1024]{1,0:T(8,128)(2,1)S(1)}, bf16[96,1024]{1,0:T(8,128)(2,1)S(1)}, u32[]{:S(2)}, u32[]{:S(2)}) %collective-permute-start.4) | collective-permute-done | bytes 196640 | tf_op jit(solution)/shard_map/ppermute | solution.py:21
  41.7 2.4 %convolution_convert_fusion.2 = bf16[96,1792]{1,0:T(8,128)(2,1)S(1)} fusion(bf16[1792,2048]{1,0:T(8,128)(2,1)S(1)} %bitcast.42, bf16[96,1024]{1,0:T(8,128)(2,1)S(1)} %get-tuple-element.35, bf16[96,1024]{1,0:T(8,128)(2,1)S(1)} %get-tuple-element.34), kind=kOutput, calls=%fused_computation.3 | convolution fusion | flops 705601536 | bytes 8077312 | tf_op jit(solution)/shard_map/dot_general | solution.py:16
  44.1 2.4 %collective-permute-start.12 = (bf16[24,1792]{1,0:T(8,128)(2,1)S(1)}, bf16[24,1792]{1,0:T(8,128)(2,1)S(1)}, u32[]{:S(2)}, u32[]{:S(2)}) collective-permute-start(bf16[24,1792]{1,0:T(8,128)(2,1)S(1)} %get-tuple-element.45), channel_id=1, source_target_pairs={{0,4},{4,0},{8,12},{12,8},{1,5},{5,1},{9,13},{13,9},{2,6},{6,2},{1... | collective-permute-start | bytes 258056 | tf_op jit(solution)/shard_map/ppermute | solution.py:21
  46.4 2.1 %collective-permute-start.13 = (bf16[24,1792]{1,0:T(8,128)(2,1)S(1)}, bf16[24,1792]{1,0:T(8,128)(2,1)S(1)}, u32[]{:S(2)}, u32[]{:S(2)}) collective-permute-start(bf16[24,1792]{1,0:T(8,128)(2,1)S(1)} %get-tuple-element.44), channel_id=1, source_target_pairs={{0,8},{4,12},{8,0},{12,4},{1,9},{5,13},{9,1},{13,5},{2,10},{6,14},... | collective-permute-start | bytes 258056 | tf_op jit(solution)/shard_map/ppermute | solution.py:21
  48.5 1.4 %collective-permute-start.14 = (bf16[24,1792]{1,0:T(8,128)(2,1)S(1)}, bf16[24,1792]{1,0:T(8,128)(2,1)S(1)}, u32[]{:S(2)}, u32[]{:S(2)}) collective-permute-start(bf16[24,1792]{1,0:T(8,128)(2,1)S(1)} %get-tuple-element.43), channel_id=1, source_target_pairs={{0,12},{4,8},{8,4},{12,0},{1,13},{5,9},{9,5},{13,1},{2,14},{6,10},... | collective-permute-start | bytes 258056 | tf_op jit(solution)/shard_map/ppermute | solution.py:21
  50.0 2.4 %fusion.36 = f32[96,1792]{1,0:T(8,128)S(1)} fusion(bf16[1792,2048]{1,0:T(8,128)(2,1)S(1)} %bitcast.44, bf16[96,1024]{1,0:T(8,128)(2,1)S(1)} %get-tuple-element.36, bf16[96,1024]{1,0:T(8,128)(2,1)S(1)} %get-tuple-element.37), kind=kOutput, calls=%fused_computation.97 | convolution fusion | flops 705429504 | bytes 8421376 | tf_op jit(solution)/shard_map/dot_general | solution.py:16
  52.5 2.4 %fusion = bf16[96,1792]{1,0:T(8,128)(2,1)S(1)} fusion(f32[96,1792]{1,0:T(8,128)S(1)} %fusion.36, bf16[1792,2048]{1,0:T(8,128)(2,1)S(1)} %copy-done.1, bf16[96,1024]{1,0:T(8,128)(2,1)S(1)} %get-tuple-element.31, bf16[96,1024]{1,0:T(8,128)(2,1)S(1)} %get-tuple-element.30), kind=kOutput, calls=%fused_computation.6 | convolution fusion | flops 705773568 | bytes 8765440 | tf_op jit(solution)/shard_map/dot_general | solution.py:16
  55.5 2.4 %collective-permute-start.17 = (bf16[24,1920]{1,0:T(8,128)(2,1)S(1)}, bf16[24,1920]{1,0:T(8,128)(2,1)S(1)}, u32[]{:S(2)}, u32[]{:S(2)}) collective-permute-start(bf16[24,1920]{1,0:T(8,128)(2,1)S(1)} %get-tuple-element.41), channel_id=1, source_target_pairs={{0,8},{4,12},{8,0},{12,4},{1,9},{5,13},{9,1},{13,5},{2,10},{6,14},... | collective-permute-start | bytes 276488 | tf_op jit(solution)/shard_map/ppermute | solution.py:21
  57.9 1.4 %collective-permute-start.18 = (bf16[24,1920]{1,0:T(8,128)(2,1)S(1)}, bf16[24,1920]{1,0:T(8,128)(2,1)S(1)}, u32[]{:S(2)}, u32[]{:S(2)}) collective-permute-start(bf16[24,1920]{1,0:T(8,128)(2,1)S(1)} %get-tuple-element.40), channel_id=1, source_target_pairs={{0,12},{4,8},{8,4},{12,0},{1,13},{5,9},{9,5},{13,1},{2,14},{6,10},... | collective-permute-start | bytes 276488 | tf_op jit(solution)/shard_map/ppermute | solution.py:21
  59.3 1.3 %convolution_convert_fusion.1 = bf16[256,1792]{1,0:T(8,128)(2,1)} fusion(bf16[96,256]{1,0:T(8,128)(2,1)S(1)} %fusion.12, bf16[24,1792]{1,0:T(8,128)(2,1)S(1)} %collective-permute-done.14, bf16[24,1792]{1,0:T(8,128)(2,1)S(1)} %collective-permute-done.13, bf16[24,1792]{1,0:T(8,128)(2,1)S(1)} %collective-permute-done.12, bf16[24,1792]{1,0:T(8,128)(2,1)S(1)} %get-tuple-element.42), kind=kOutput, calls=%fused_computation.1 | convolution fusion | flops 89915392 | bytes 1310720 | tf_op jit(solution)/shard_map/dot_general | solution.py:16
  60.7 5.8 %shard_map.118 = (bf16[1792,2048]{1,0:T(8,128)(2,1)}, bf16[1792,2048]{1,0:T(8,128)(2,1)}) custom-call(bf16[96,1792]{1,0:T(8,128)(2,1)S(1)} %pad_maximum_fusion.7.rows_ref, bf16[96,2048]{1,0:T(8,128)(2,1)S(1)} %pad_maximum_fusion.2.refs_0_, bf16[96,2048]{1,0:T(8,128)(2,1)S(1)} %pad_maximum_fusion.3.refs_1_), custom_call_target="tpu_custom_call" | custom-call | flops 1409286144 | bytes 14680064 | tf_op jit(solution)/shard_map/pallas_call | solution.py:73
  66.5 3.4 %shard_map.119 = bf16[1792,2048]{1,0:T(8,128)(2,1)} custom-call(bf16[96,1792]{1,0:T(8,128)(2,1)S(1)} %pad_maximum_fusion.6.rows_ref, bf16[96,2048]{1,0:T(8,128)(2,1)S(1)} %pad_maximum_fusion.4.refs_0_), custom_call_target="tpu_custom_call" | custom-call | flops 704643072 | bytes 7340032 | tf_op jit(solution)/shard_map/pallas_call | solution.py:73
  71.0 1.4 %convolution_convert_fusion = bf16[256,1792]{1,0:T(8,128)(2,1)} fusion(pred[96,256]{1,0:T(32,128)(4,1)S(1)} %fusion.13, bf16[96,1920]{1,0:T(8,128)(2,1)S(1)} %pad_maximum_fusion.5), kind=kOutput, calls=%fused_computation | convolution fusion | flops 88539136 | bytes 1286144 | tf_op jit(solution)/shard_map/dot_general | solution.py:16
  (79 shorter events, 8.6 us)
Async XLA Ops:
  1.8 18.4 %copy-start.1 = (bf16[1792,2048]{1,0:T(8,128)(2,1)S(1)}, bf16[1792,2048]{1,0:T(8,128)(2,1)}, u32[]{:S(2)}) copy-start(bf16[1792,2048]{1,0:T(8,128)(2,1)} %param.11) | copy-start | bytes 22020100
  2.2 13.2 %collective-permute-start.5 = (bf16[24,1792]{1,0:T(8,128)(2,1)S(1)}, bf16[24,1792]{1,0:T(8,128)(2,1)S(1)}, u32[]{:S(2)}, u32[]{:S(2)}) collective-permute-start(bf16[24,1792]{1,0:T(8,128)(2,1)S(1)} %get-tuple-element.49), channel_id=1, source_target_pairs={{0,4},{4,0},{8,12},{12,8},{1,5},{5,1},{9,13},{13,9},{2,6},{6,2},{1... | collective-permute-start | bytes 258056 | tf_op jit(solution)/shard_map/ppermute | solution.py:21
  5.3 10.2 %collective-permute-start.6 = (bf16[24,1792]{1,0:T(8,128)(2,1)S(1)}, bf16[24,1792]{1,0:T(8,128)(2,1)S(1)}, u32[]{:S(2)}, u32[]{:S(2)}) collective-permute-start(bf16[24,1792]{1,0:T(8,128)(2,1)S(1)} %get-tuple-element.48), channel_id=1, source_target_pairs={{0,8},{4,12},{8,0},{12,4},{1,9},{5,13},{9,1},{13,5},{2,10},{6,14},... | collective-permute-start | bytes 258056 | tf_op jit(solution)/shard_map/ppermute | solution.py:21
  7.9 7.7 %collective-permute-start.7 = (bf16[24,1792]{1,0:T(8,128)(2,1)S(1)}, bf16[24,1792]{1,0:T(8,128)(2,1)S(1)}, u32[]{:S(2)}, u32[]{:S(2)}) collective-permute-start(bf16[24,1792]{1,0:T(8,128)(2,1)S(1)} %get-tuple-element.47), channel_id=1, source_target_pairs={{0,12},{4,8},{8,4},{12,0},{1,13},{5,9},{9,5},{13,1},{2,14},{6,10},... | collective-permute-start | bytes 258056 | tf_op jit(solution)/shard_map/ppermute | solution.py:21
  11.0 10.8 %collective-permute-start = (bf16[24,1792]{1,0:T(8,128)(2,1)S(1)}, bf16[24,1792]{1,0:T(8,128)(2,1)S(1)}, u32[]{:S(2)}, u32[]{:S(2)}) collective-permute-start(bf16[24,1792]{1,0:T(8,128)(2,1)S(1)} %get-tuple-element.53), channel_id=1, source_target_pairs={{0,4},{4,0},{8,12},{12,8},{1,5},{5,1},{9,13},{13,9},{2,6},{6,2},{1... | collective-permute-start | bytes 258056 | tf_op jit(solution)/shard_map/ppermute | solution.py:21
  11.9 10.0 %collective-permute-start.1 = (bf16[24,1792]{1,0:T(8,128)(2,1)S(1)}, bf16[24,1792]{1,0:T(8,128)(2,1)S(1)}, u32[]{:S(2)}, u32[]{:S(2)}) collective-permute-start(bf16[24,1792]{1,0:T(8,128)(2,1)S(1)} %get-tuple-element.52), channel_id=1, source_target_pairs={{0,8},{4,12},{8,0},{12,4},{1,9},{5,13},{9,1},{13,5},{2,10},{6,14},... | collective-permute-start | bytes 258056 | tf_op jit(solution)/shard_map/ppermute | solution.py:21
  15.5 6.5 %collective-permute-start.2 = (bf16[24,1792]{1,0:T(8,128)(2,1)S(1)}, bf16[24,1792]{1,0:T(8,128)(2,1)S(1)}, u32[]{:S(2)}, u32[]{:S(2)}) collective-permute-start(bf16[24,1792]{1,0:T(8,128)(2,1)S(1)} %get-tuple-element.51), channel_id=1, source_target_pairs={{0,12},{4,8},{8,4},{12,0},{1,13},{5,9},{9,5},{13,1},{2,14},{6,10},... | collective-permute-start | bytes 258056 | tf_op jit(solution)/shard_map/ppermute | solution.py:21
  15.6 6.4 %slice-start = ((s8[7340032]{0:T(1024)(128)(4,1)}), s8[4194304]{0:T(1024)(128)(4,1)S(1)}, s32[]{:S(2)}) async-start(s8[7340032]{0:T(1024)(128)(4,1)} %bitcast.41), calls=%async_computation | async-start | bytes 8388608
  21.7 2.4 %collective-permute-start.8 = (f32[96,2048]{1,0:T(8,128)S(1)}, f32[96,2048]{1,0:T(8,128)S(1)}, u32[]{:S(2)}, u32[]{:S(2)}) collective-permute-start(f32[96,2048]{1,0:T(8,128)S(1)} %pad_maximum_fusion), channel_id=1, source_target_pairs={{0,1},{1,0},{2,3},{3,2},{4,5},{5,4},{6,7},{7,6},{8,9},{9,8},{10,11... | collective-permute-start | bytes 2359304 | tf_op jit(solution)/shard_map/ppermute | solution.py:21
  23.4 2.5 %collective-permute-start.3 = (f32[96,1024]{1,0:T(8,128)S(1)}, f32[96,1024]{1,0:T(8,128)S(1)}, u32[]{:S(2)}, u32[]{:S(2)}) collective-permute-start(f32[96,1024]{1,0:T(8,128)S(1)} %slice_select_fusion.4), channel_id=1, source_target_pairs={{0,1},{1,0},{2,3},{3,2},{4,5},{5,4},{6,7},{7,6},{8,9},{9,8},{10,11... | collective-permute-start | bytes 1179656 | tf_op jit(solution)/shard_map/ppermute | solution.py:21
  24.2 12.0 %collective-permute-start.9 = (bf16[96,2048]{1,0:T(8,128)(2,1)S(1)}, bf16[96,2048]{1,0:T(8,128)(2,1)S(1)}, u32[]{:S(2)}, u32[]{:S(2)}) collective-permute-start(bf16[96,2048]{1,0:T(8,128)(2,1)S(1)} %fusion.11), channel_id=1, source_target_pairs={{0,2},{1,3},{2,0},{3,1},{4,6},{5,7},{6,4},{7,5},{8,10},{9,11},{10,... | collective-permute-start | bytes 1179656 | tf_op jit(solution)/shard_map/ppermute | solution.py:21
  26.0 13.6 %collective-permute-start.4 = (bf16[96,1024]{1,0:T(8,128)(2,1)S(1)}, bf16[96,1024]{1,0:T(8,128)(2,1)S(1)}, u32[]{:S(2)}, u32[]{:S(2)}) collective-permute-start(bf16[96,1024]{1,0:T(8,128)(2,1)S(1)} %get-tuple-element.22), channel_id=1, source_target_pairs={{0,2},{1,3},{2,0},{3,1},{4,6},{5,7},{6,4},{7,5},{8,10},{9,11},{10,... | collective-permute-start | bytes 589832 | tf_op jit(solution)/shard_map/ppermute | solution.py:21
  39.6 10.4 %slice-start.2 = ((s8[7340032]{0:T(1024)(128)(4,1)}), s8[4194304]{0:T(1024)(128)(4,1)S(1)}, s32[]{:S(2)}) async-start(s8[7340032]{0:T(1024)(128)(4,1)} %bitcast.43), calls=%async_computation.2 | async-start | bytes 8388608
  40.0 1.6 %collective-permute-start.11 = (bf16[96,1024]{1,0:T(8,128)(2,1)S(1)}, bf16[96,1024]{1,0:T(8,128)(2,1)S(1)}, u32[]{:S(2)}, u32[]{:S(2)}) collective-permute-start(bf16[96,1024]{1,0:T(8,128)(2,1)S(1)} %get-tuple-element.21), channel_id=1, source_target_pairs={{0,1},{1,0},{2,3},{3,2},{4,5},{5,4},{6,7},{7,6},{8,9},{9,8},{10,11... | collective-permute-start | bytes 589832 | tf_op jit(solution)/shard_map/ppermute | solution.py:21
  40.1 1.4 %collective-permute-start.15 = (f32[96,1]{0,1:T(1,128)S(1)}, f32[96,1]{0,1:T(1,128)S(1)}, u32[]{:S(2)}, u32[]{:S(2)}) collective-permute-start(f32[96,1]{0,1:T(1,128)S(1)} %bitcast.49), channel_id=1, source_target_pairs={{0,1},{1,0},{2,3},{3,2},{4,5},{5,4},{6,7},{7,6},{8,9},{9,8},{10,11... | collective-permute-start | bytes 1160 | tf_op jit(solution)/shard_map/ppermute | solution.py:21
  40.6 9.3 %collective-permute-start.10 = (bf16[96,2048]{1,0:T(8,128)(2,1)S(1)}, bf16[96,2048]{1,0:T(8,128)(2,1)S(1)}, u32[]{:S(2)}, u32[]{:S(2)}) collective-permute-start(bf16[96,2048]{1,0:T(8,128)(2,1)S(1)} %pad_maximum_fusion.1), channel_id=1, source_target_pairs={{0,1},{1,0},{2,3},{3,2},{4,5},{5,4},{6,7},{7,6},{8,9},{9,8},{10,11... | collective-permute-start | bytes 1179656 | tf_op jit(solution)/shard_map/ppermute | solution.py:21
  41.7 8.3 %slice-start.3 = ((s8[7340032]{0:T(1024)(128)(4,1)}), s8[3145728]{0:T(1024)(128)(4,1)S(1)}, s32[]{:S(2)}) async-start(s8[7340032]{0:T(1024)(128)(4,1)} %bitcast.43), calls=%async_computation.3 | async-start | bytes 6291456
  44.1 13.9 %collective-permute-start.12 = (bf16[24,1792]{1,0:T(8,128)(2,1)S(1)}, bf16[24,1792]{1,0:T(8,128)(2,1)S(1)}, u32[]{:S(2)}, u32[]{:S(2)}) collective-permute-start(bf16[24,1792]{1,0:T(8,128)(2,1)S(1)} %get-tuple-element.45), channel_id=1, source_target_pairs={{0,4},{4,0},{8,12},{12,8},{1,5},{5,1},{9,13},{13,9},{2,6},{6,2},{1... | collective-permute-start | bytes 258056 | tf_op jit(solution)/shard_map/ppermute | solution.py:21
  46.4 12.9 %collective-permute-start.13 = (bf16[24,1792]{1,0:T(8,128)(2,1)S(1)}, bf16[24,1792]{1,0:T(8,128)(2,1)S(1)}, u32[]{:S(2)}, u32[]{:S(2)}) collective-permute-start(bf16[24,1792]{1,0:T(8,128)(2,1)S(1)} %get-tuple-element.44), channel_id=1, source_target_pairs={{0,8},{4,12},{8,0},{12,4},{1,9},{5,13},{9,1},{13,5},{2,10},{6,14},... | collective-permute-start | bytes 258056 | tf_op jit(solution)/shard_map/ppermute | solution.py:21
  48.5 10.8 %collective-permute-start.14 = (bf16[24,1792]{1,0:T(8,128)(2,1)S(1)}, bf16[24,1792]{1,0:T(8,128)(2,1)S(1)}, u32[]{:S(2)}, u32[]{:S(2)}) collective-permute-start(bf16[24,1792]{1,0:T(8,128)(2,1)S(1)} %get-tuple-element.43), channel_id=1, source_target_pairs={{0,12},{4,8},{8,4},{12,0},{1,13},{5,9},{9,5},{13,1},{2,14},{6,10},... | collective-permute-start | bytes 258056 | tf_op jit(solution)/shard_map/ppermute | solution.py:21
  54.9 15.1 %collective-permute-start.16 = (bf16[24,1920]{1,0:T(8,128)(2,1)S(1)}, bf16[24,1920]{1,0:T(8,128)(2,1)S(1)}, u32[]{:S(2)}, u32[]{:S(2)}) collective-permute-start(bf16[24,1920]{1,0:T(8,128)(2,1)S(1)} %get-tuple-element.39), channel_id=1, source_target_pairs={{0,4},{4,0},{8,12},{12,8},{1,5},{5,1},{9,13},{13,9},{2,6},{6,2},{1... | collective-permute-start | bytes 276488 | tf_op jit(solution)/shard_map/ppermute | solution.py:21
  55.5 14.5 %collective-permute-start.17 = (bf16[24,1920]{1,0:T(8,128)(2,1)S(1)}, bf16[24,1920]{1,0:T(8,128)(2,1)S(1)}, u32[]{:S(2)}, u32[]{:S(2)}) collective-permute-start(bf16[24,1920]{1,0:T(8,128)(2,1)S(1)} %get-tuple-element.41), channel_id=1, source_target_pairs={{0,8},{4,12},{8,0},{12,4},{1,9},{5,13},{9,1},{13,5},{2,10},{6,14},... | collective-permute-start | bytes 276488 | tf_op jit(solution)/shard_map/ppermute | solution.py:21
  57.9 12.0 %collective-permute-start.18 = (bf16[24,1920]{1,0:T(8,128)(2,1)S(1)}, bf16[24,1920]{1,0:T(8,128)(2,1)S(1)}, u32[]{:S(2)}, u32[]{:S(2)}) collective-permute-start(bf16[24,1920]{1,0:T(8,128)(2,1)S(1)} %get-tuple-element.40), channel_id=1, source_target_pairs={{0,12},{4,8},{8,4},{12,0},{1,13},{5,9},{9,5},{13,1},{2,14},{6,10},... | collective-permute-start | bytes 276488 | tf_op jit(solution)/shard_map/ppermute | solution.py:21
  59.3 10.9 %copy-start.2 = (s32[256,8]{0,1:T(8,128)S(1)}, s32[256,8]{0,1:T(8,128)}, u32[]{:S(2)}) copy-start(s32[256,8]{0,1:T(8,128)} %param.9) | copy-start | bytes 24580
  (2 other events, 3.1 us)

commit v3 on v2

v3 whole, which is shorter than its diff:
```python
import jax
import jax.numpy as jnp
from jax import lax
from jax.experimental import pallas as pl
from jax.experimental.pallas import tpu as pltpu
from jax.sharding import PartitionSpec as P

EXPERTS = 4
CAP = 24
EXTRA = 128
BF = jnp.bfloat16
F32 = jnp.float32


def dot(left, right, dims):
    return lax.dot_general(left, right, (dims, ((), ())), preferred_element_type=F32)


def swap(value, axis, step):
    size = lax.axis_size(axis)
    return lax.ppermute(value, axis, [(i, i ^ step) for i in range(size)])


def exchange(blocks, axis, last=1):
    size = len(blocks)
    got = {0: blocks[0]}
    for step in sorted(range(1, size), key=lambda step: (step == last, step)):
        got[step] = swap(blocks[step], axis, step)
    return [got[step] for step in range(size)]


def held(value):
    return pltpu.with_memory_space_constraint(value, pltpu.VMEM)


def project(rows, weight):
    hidden = weight.shape[1]
    tile = min(512, hidden)

    def body(rows_ref, weight_ref, out_ref):
        values = rows_ref[...]
        for at in range(0, hidden, tile):
            out_ref[:, at:at + tile] = dot(values, weight_ref[:, at:at + tile], ((1,), (0,)))

    vmem = pl.BlockSpec(memory_space=pltpu.VMEM)
    flops = 2 * rows.shape[0] * weight.shape[0] * hidden
    return pl.pallas_call(
        body,
        in_specs=[vmem, vmem],
        out_specs=vmem,
        out_shape=jax.ShapeDtypeStruct((rows.shape[0], hidden), F32),
        compiler_params=pltpu.CompilerParams(vmem_limit_bytes=5 << 20),
        cost_estimate=pl.CostEstimate(flops=flops, bytes_accessed=1 << 20, transcendentals=0),
    )(rows, held(weight))


def split_rows(packed, refs):
    if len(refs) == 1:
        refs[0][...] = packed.astype(BF)
        return
    for s, ref in enumerate(refs):
        ref[...] = packed[s * CAP:(s + 1) * CAP].astype(BF)


def pack_shapes(blocks, split, width):
    if split:
        return [jax.ShapeDtypeStruct((CAP, width), BF)] * blocks
    return [jax.ShapeDtypeStruct((blocks * CAP, width), BF)]


def in_hbm(value):
    return pltpu.with_memory_space_constraint(value, pltpu.HBM)


def route(labels, ids, gates, tokens, blocks, split):
    count = ids.shape[1]
    total = blocks * CAP
    pad = max(8, blocks)
    packs = pack_shapes(blocks, split, tokens.shape[1])

    def body(labels_ref, ids_hbm, gates_hbm, tokens_hbm, pick_ref, pick_w_ref, *refs):
        outs, (ids_ref, gates_ref, tokens_ref, sem) = refs[:-4], refs[-4:]
        copies = [
            pltpu.make_async_copy(src, dst, sem.at[i])
            for i, (src, dst) in enumerate(
                ((ids_hbm, ids_ref), (gates_hbm, gates_ref), (tokens_hbm, tokens_ref)))
        ]
        for copy in copies:
            copy.start()
        copies[0].wait()
        copies[1].wait()
        ids_v = ids_ref[...]
        gates_v = gates_ref[...].astype(F32)
        row = lax.broadcasted_iota(jnp.int32, (pad, count), 0)
        member = jnp.zeros((pad, count), F32)
        found, weights = [], []
        for s in range(blocks):
            match = ids_v == labels_ref[s]
            found.append(jnp.max(jnp.where(match, 1.0, 0.0), axis=0, keepdims=True))
            weights.append(jnp.sum(jnp.where(match, gates_v, 0.0), axis=0, keepdims=True))
            member = jnp.where(row == s, found[s], member)
        left = lax.broadcasted_iota(jnp.int32, (count, count), 0)
        right = lax.broadcasted_iota(jnp.int32, (count, count), 1)
        earlier = jnp.where(left < right, 1.0, 0.0).astype(BF)
        slot = dot(member.astype(BF), earlier, ((1,), (0,)))
        place = lax.broadcasted_iota(jnp.int32, (CAP, count), 0).astype(F32)
        plain, weighted = [], []
        for s in range(blocks):
            chosen = jnp.where(slot[s:s + 1] == place, found[s], 0.0)
            plain.append(chosen)
            weighted.append(chosen * weights[s])
        pick = jnp.concatenate(plain, axis=0).astype(BF)
        pick_ref[...] = pick
        pick_w_ref[...] = jnp.concatenate(weighted, axis=0).astype(BF)
        copies[2].wait()
        split_rows(dot(pick, tokens_ref[...], ((1,), (0,))), outs)

    vmem = pl.BlockSpec(memory_space=pltpu.VMEM)
    hbm = pl.BlockSpec(memory_space=pltpu.HBM)
    out = pl.pallas_call(
        body,
        in_specs=[pl.BlockSpec(memory_space=pltpu.SMEM)] + [hbm] * 3,
        out_specs=[vmem] * (2 + len(packs)),
        out_shape=[jax.ShapeDtypeStruct((total, count), BF)] * 2 + packs,
        scratch_shapes=[
            pltpu.VMEM(ids.shape, ids.dtype),
            pltpu.VMEM(gates.shape, gates.dtype),
            pltpu.VMEM(tokens.shape, tokens.dtype),
            pltpu.SemaphoreType.DMA((3,)),
        ],
        compiler_params=pltpu.CompilerParams(vmem_limit_bytes=10 << 20),
        cost_estimate=pl.CostEstimate(flops=1 << 34, bytes_accessed=1 << 20, transcendentals=0),
    )(labels, in_hbm(ids), in_hbm(gates), in_hbm(tokens))
    return out[0], out[1], list(out[2:])


def pack_cotangent(pick_w, cotangent, after, blocks, split):
    packs = pack_shapes(blocks, split, cotangent.shape[1])

    def body(pick_ref, cot_ref, after_ref, *outs):
        split_rows(dot(pick_ref[...], cot_ref[...], ((1,), (0,))), outs)

    vmem = pl.BlockSpec(memory_space=pltpu.VMEM)
    out = pl.pallas_call(
        body,
        in_specs=[vmem, vmem, pl.BlockSpec(memory_space=pl.ANY)],
        out_specs=[vmem] * len(packs),
        out_shape=packs,
        compiler_params=pltpu.CompilerParams(vmem_limit_bytes=8 << 20),
        cost_estimate=pl.CostEstimate(flops=1 << 20, bytes_accessed=1 << 10, transcendentals=0),
    )(pick_w, cotangent, after)
    return list(out)


def send_columns(mat, values, buf, out, sem, width):
    block = width // 2 if width % 256 == 0 else width
    for at in range(0, width, block):
        buf[:, at:at + block] = dot(mat, values[:, at:at + block], ((0,), (0,))).astype(BF)
        pltpu.make_async_copy(buf.at[:, pl.ds(at, block)], out.at[:, pl.ds(at, block)], sem).start()


def finish(labels, ids, gates, pick, back):
    total, count = pick.shape
    blocks = total // CAP
    width = back.shape[1] - EXTRA

    def body(labels_ref, ids_ref, gates_ref, pick_ref, back_ref, out, gate_grad_ref, buf, sem):
        mat = pick_ref[...]
        send_columns(mat, back_ref, buf, out, sem, width)
        source = lax.broadcasted_iota(jnp.int32, (total, EXTRA), 0) // CAP
        lane = lax.broadcasted_iota(jnp.int32, (total, EXTRA), 1) % (EXTRA // 2)
        extra = back_ref[:, width:].astype(F32)
        placed = jnp.where(source == lane, extra, 0.0).astype(BF)
        score = dot(placed, mat, ((0,), (0,)))
        score = score[:EXTRA // 2] + score[EXTRA // 2:]
        ids_v = ids_ref[...]
        grad = jnp.zeros(ids_v.shape, F32)
        for s in range(blocks):
            grad = grad + jnp.where(ids_v == labels_ref[s], score[s:s + 1], 0.0)
        gate_grad_ref[...] = (grad / gates_ref[...].astype(F32)).astype(BF)
        pltpu.make_async_copy(buf, out, sem).wait()

    vmem = pl.BlockSpec(memory_space=pltpu.VMEM)
    return pl.pallas_call(
        body,
        in_specs=[pl.BlockSpec(memory_space=pltpu.SMEM)] + [vmem] * 4,
        out_specs=[pl.BlockSpec(memory_space=pl.ANY), vmem],
        out_shape=[jax.ShapeDtypeStruct((count, width), BF), jax.ShapeDtypeStruct(ids.shape, BF)],
        scratch_shapes=[pltpu.VMEM((count, width), BF), pltpu.SemaphoreType.DMA],
        compiler_params=pltpu.CompilerParams(vmem_limit_bytes=10 << 20),
        cost_estimate=pl.CostEstimate(flops=1 << 20, bytes_accessed=1 << 20, transcendentals=0),
    )(labels, ids, gates, pick, back)


def core_sum(value, even):
    half = value.shape[1] // 2
    mine = jnp.where(even, value[:, :half], value[:, half:])
    other = jnp.where(even, value[:, half:], value[:, :half])
    return mine + swap(other, "dp", 1)


def first_swap(total):
    return swap(total.astype(BF), "dp", 2)


def chip_sum(total, got):
    total = total + got.astype(F32)
    step = 4
    while step < lax.axis_size("dp"):
        total = total + swap(total.astype(BF), "dp", step).astype(F32)
        step *= 2
    return total


def join(values, even):
    half = values[0].shape[1]
    other = swap(jnp.concatenate(values, axis=1), "dp", 1)
    out = []
    for i, v in enumerate(values):
        o = other[:, i * half:(i + 1) * half]
        out.append(jnp.concatenate([jnp.where(even, v, o), jnp.where(even, o, v)], axis=1))
    return out


def weight_grads(rows, cots, pick_w=None, back=None):
    count, width = rows.shape
    hidden = cots[0].shape[1]
    n = len(cots)
    block = 256 if width % 256 == 0 else 128
    combine = pick_w is not None

    def body(*refs):
        rows_ref, cot_refs, refs = refs[0], refs[1:1 + n], refs[1 + n:]
        if combine:
            pick_ref, back_ref, refs = refs[0], refs[1], refs[2:]
        outs, bufs, sem = refs[:n + combine], refs[n + combine:-1], refs[-1]
        if combine:
            send_columns(pick_ref[...], back_ref, bufs[n], outs[n], sem.at[n], width)
        values = [c[...] for c in cot_refs]
        for at in range(0, width, block):
            part = rows_ref[:, at:at + block]
            for i in range(n):
                bufs[i][at:at + block, :] = dot(part, values[i], ((0,), (0,))).astype(BF)
                pltpu.make_async_copy(
                    bufs[i].at[pl.ds(at, block)], outs[i].at[pl.ds(at, block)], sem.at[i]
                ).start()
        for i in range(n + combine):
            pltpu.make_async_copy(bufs[i], outs[i], sem.at[i]).wait()

    shapes = [(width, hidden)] * n + ([(pick_w.shape[1], width)] if combine else [])
    size = n * width * hidden * 2
    vmem = pl.BlockSpec(memory_space=pltpu.VMEM)
    operands = [rows, *cots] + ([pick_w, back] if combine else [])
    return pl.pallas_call(
        body,
        in_specs=[vmem] * len(operands),
        out_specs=[pl.BlockSpec(memory_space=pl.ANY)] * len(shapes),
        out_shape=[jax.ShapeDtypeStruct(shape, BF) for shape in shapes],
        scratch_shapes=[pltpu.VMEM(shape, BF) for shape in shapes]
        + [pltpu.SemaphoreType.DMA((len(shapes),))],
        compiler_params=pltpu.CompilerParams(vmem_limit_bytes=size + (10 << 20)),
        cost_estimate=pl.CostEstimate(flops=size * count, bytes_accessed=size, transcendentals=0),
    )(*operands)


def per_device(tokens, cotangent, expert_ids, gate_values, w_gate, w_up, w_down):
    devices = lax.axis_size("expert")
    span = devices // EXPERTS
    count, width = tokens.shape
    direct = devices <= 8
    even = lax.axis_index("dp") % 2 == 0
    me = lax.axis_index("expert")
    expert_ids, even, me = lax.optimization_barrier((expert_ids, even, me))

    steps = jnp.arange(devices, dtype=jnp.int32)
    labels = ((steps ^ me) if direct else steps) // span
    ids, gates = expert_ids.T, gate_values.T
    pick, pick_w, packed_x = route(labels, ids, gates, tokens, devices, direct)

    def move(blocks):
        if direct:
            return jnp.concatenate(exchange(blocks, "expert"), axis=0)
        rows = jnp.concatenate(blocks, axis=0) if len(blocks) > 1 else blocks[0]
        got = lax.all_to_all(rows.reshape(devices, CAP, -1), "expert", split_axis=0, concat_axis=0, tiled=True)
        return got.reshape(devices * CAP, -1)

    def cut(rows):
        return [rows[s * CAP:(s + 1) * CAP] for s in range(devices)] if direct else [rows]

    if direct:
        got = exchange(packed_x, "expert")
        rows = jnp.concatenate(got, axis=0)
    else:
        rows = move(packed_x)
    gate = core_sum(project(rows, w_gate), even)
    up = core_sum(project(rows, w_up), even)
    gate_swap, up_swap = first_swap(gate), first_swap(up)
    packed_g = pack_cotangent(pick_w, cotangent, up, devices, direct)
    packed_g = exchange(packed_g, "expert") if direct else [move(packed_g)]
    grads = jnp.concatenate(packed_g, axis=0)
    gate, up, grads = lax.optimization_barrier((gate, up, grads))
    hidden_grad = core_sum(project(grads, w_down), even)
    grad_swap = first_swap(hidden_grad)
    gate = chip_sum(gate, gate_swap)
    up = chip_sum(up, up_swap)
    sigma = jax.nn.sigmoid(gate)
    active = gate * sigma
    hidden_h, gate, up, sigma, active, hidden_grad = lax.optimization_barrier(
        ((active * up).astype(BF), gate, up, sigma, active, hidden_grad))
    (hidden,) = join([hidden_h], even)
    part_out = dot(hidden, w_down, ((1,), (1,))).astype(BF)
    hidden_grad = chip_sum(hidden_grad, grad_swap)
    d_up = (hidden_grad * active).astype(BF)
    d_gate = (hidden_grad * up * sigma * (1.0 + gate * (1.0 - sigma))).astype(BF)
    (grad_down,) = weight_grads(grads, [hidden])
    part_out, d_up, d_gate, grad_down = lax.optimization_barrier((part_out, d_up, d_gate, grad_down))
    back_out = exchange(cut(part_out), "expert") if direct else [move(cut(part_out))]
    d_up, d_gate = join([d_up, d_gate], even)
    score = jnp.sum(hidden_grad * hidden_h.astype(F32), axis=1, keepdims=True)
    score = score + swap(score, "dp", 1)
    step = 2
    while step < lax.axis_size("dp"):
        score = 0.5 * (score + swap(score, "dp", step))
        step *= 2
    high = lax.reduce_precision(score, 8, 7)
    low = (score - high).astype(BF)
    high = high.astype(BF)
    lanes = jnp.arange(EXTRA)[None, :]
    extra = jnp.where(lanes < EXTRA // 2, high, low)
    part_in = (dot(d_gate, w_gate, ((1,), (1,))) + dot(d_up, w_up, ((1,), (1,)))).astype(BF)
    back_in = move(cut(jnp.concatenate([part_in, extra], axis=1)))

    late_w, back_out[0] = lax.optimization_barrier((pick_w, back_out[0], part_in))[:2]
    back_out = jnp.concatenate(back_out, axis=0)
    grad_gate, grad_up, output = weight_grads(rows, [d_gate, d_up], late_w, back_out)
    input_grad, gate_grad = finish(labels, ids, gates, pick, back_in)
    return output, input_grad, gate_grad.T, grad_gate, grad_up, grad_down


def solution(mesh):
    in_specs = (
        P(("groups", "expert"), "dp"),
        P(("groups", "expert"), "dp"),
        P(("groups", "expert"), None),
        P(("groups", "expert"), None),
        P("dp", "expert"),
        P("dp", "expert"),
        P("dp", "expert"),
    )
    out_specs = (
        P(("groups", "expert"), "dp"),
        P(("groups", "expert"), "dp"),
        P(("groups", "expert"), None),
        P(("groups", "dp"), "expert"),
        P(("groups", "dp"), "expert"),
        P(("groups", "dp"), "expert"),
    )
    return jax.shard_map(
        per_device, mesh=mesh, in_specs=in_specs, out_specs=out_specs, check_vma=False
    )
```

time: 72.7 us -> 68 us (0.935)
  matrix products: 19.2 us -> 7.3 us
  Pallas kernels: 9.26 us -> 18.4 us
  other arithmetic: 4.58 us -> 1.42 us
  starting transfers between devices: 24.4 us -> 25.4 us
    dot_general x12 -> x3, matrix products: 19.2 us -> 7.3 us  [dot(): lax.dot_general(left, right, (dims, ((), ())), preferred_element_type=F32)]
    pallas_call x2 -> x8, Pallas kernels: 9.26 us -> 18.4 us  [the longest x2 9.36 us: weight_grads(): pl.pallas_call(body, in_specs=[vmem] * len(operands), out_specs=[pl.Block...]
    reduce_sum x2 -> x0, other arithmetic: 1.45 us -> none  [the longest x1 0.78 us: per_device(): jnp.sum(jnp.where(match, gate_values.T.astype(F32)[None], 0.0), axis=1)]
    ppermute x19 -> x22, starting transfers between devices: 24.4 us -> 25.4 us  [swap(): return lax.ppermute(value, axis, [(i, i ^ step) for i in range(size)])]
    reduce_or x1 -> x0, other arithmetic: 0.86 us -> none  [per_device(): member = jnp.any(match, axis=1)]
    ppermute x19 -> x22, waiting for transfers between devices: 13.6 us -> 14 us  [swap(): return lax.ppermute(value, axis, [(i, i ^ step) for i in range(size)])]
  transfers between devices with their start and end apart: 19 -> 22, of which waited for: 5 -> 5; matrix products, arithmetic and copies ran while one was open for 27% -> 12% of each run, Pallas kernels for 13% -> 18%
where the time goes in v3:
time: 68 us; the launch traced here: 67.8 us
  starting transfers between devices  25.4 us (37%)
  Pallas kernels  18.4 us (27%)
  waiting for transfers between devices  14 us (21%)
  matrix products  7.3 us (11%)
  other arithmetic  1.42 us (2%)
  between operations  1.26 us (2%)
    ppermute x22, starting transfers between devices, swap(): return lax.ppermute(value, axis, [(i, i ^ step) for i in range(size)])  25.4 us
    ppermute x22, waiting for transfers between devices, swap(): return lax.ppermute(value, axis, [(i, i ^ step) for i in range(size)])  14 us
    pallas_call x2, Pallas kernels, weight_grads(): pl.pallas_call(body, in_specs=[vmem] * len(operands), out_specs=[pl.Block...  9.36 us
    dot_general x3, matrix products, dot(): lax.dot_general(left, right, (dims, ((), ())), preferred_element_type=F32)  7.3 us
    pallas_call x3, Pallas kernels, project(): pl.pallas_call(body, in_specs=[vmem, vmem], out_specs=vmem, out_shape=jax...  3.88 us
    pallas_call x1, Pallas kernels, route(): pl.pallas_call(body, in_specs=[pl.BlockSpec(memory_space=pltpu.SMEM)] + [...  2.46 us
    pallas_call x1, Pallas kernels, finish(): pl.pallas_call(body, in_specs=[pl.BlockSpec(memory_space=pltpu.SMEM)] + [...  2.38 us
  transfers between devices with their start and end apart: 22, of which 5 were waited for; matrix products, arithmetic and copies ran while one was open for 12% of the time, Pallas kernels for 18%

profile of v3, /device:TPU:0, one launch (start us, length us, event | category | flops | bytes accessed | tf_op | source)
XLA Modules:
  0.0 67.8 jit_solution(14304502156717267548)
XLA Ops:
  0.7 2.5 %shard_map.118 = (bf16[96,256]{1,0:T(8,128)(2,1)S(1)}, bf16[96,256]{1,0:T(8,128)(2,1)S(1)}, bf16[24,1792]{1,0:T(8,128)(2,1)S(1)}, bf16[24,1792]{1,0:T(8,128)(2,1...) custom-call(s32[4]{0:T(128)S(1)} %iota_xor_fusion.labels_ref, s32[8,256]{1,0:T(8,128)} %bitcast.16, ...), custom_call_target="tpu_custom_call" | custom-call | flops 17179869184 | bytes 1048576 | tf_op jit(solution)/shard_map/pallas_call | solution.py:120
  3.2 3.1 %collective-permute-start = (bf16[24,1792]{1,0:T(8,128)(2,1)S(1)}, bf16[24,1792]{1,0:T(8,128)(2,1)S(1)}, u32[]{:S(2)}, u32[]{:S(2)}) collective-permute-start(bf16[24,1792]{1,0:T(8,128)(2,1)S(1)} %get-tuple-element.42), channel_id=1, source_target_pairs={{0,4},{4,0},{8,12},{12,8},{1,5},{5,1},{9,13},{13,9},{2,6},{6,2},{1... | collective-permute-start | bytes 258056 | tf_op jit(solution)/shard_map/ppermute | solution.py:21
  6.2 2.6 %collective-permute-start.1 = (bf16[24,1792]{1,0:T(8,128)(2,1)S(1)}, bf16[24,1792]{1,0:T(8,128)(2,1)S(1)}, u32[]{:S(2)}, u32[]{:S(2)}) collective-permute-start(bf16[24,1792]{1,0:T(8,128)(2,1)S(1)} %get-tuple-element.43), channel_id=1, source_target_pairs={{0,8},{4,12},{8,0},{12,4},{1,9},{5,13},{9,1},{13,5},{2,10},{6,14},... | collective-permute-start | bytes 258056 | tf_op jit(solution)/shard_map/ppermute | solution.py:21
  8.9 6.9 %collective-permute-done.1 = bf16[24,1792]{1,0:T(8,128)(2,1)S(1)} collective-permute-done((bf16[24,1792]{1,0:T(8,128)(2,1)S(1)}, bf16[24,1792]{1,0:T(8,128)(2,1)S(1)}, u32[]{:S(2)}, u32[]{:S(2)}) %collective-permute-start.1) | collective-permute-done | bytes 86048 | tf_op jit(solution)/shard_map/ppermute | solution.py:21
  15.8 1.3 %shard_map.120 = f32[96,2048]{1,0:T(8,128)S(1)} custom-call(bf16[96,1792]{1,0:T(8,128)(2,1)S(1)} %constant_dynamic-update-slice_fusion.rows_ref.refs_0_, bf16[1792,2048]{1,0:T(8,128)(2,1)S(1)} %copy-done), custom_call_target="tpu_custom_call" | custom-call | flops 704643072 | bytes 1048576 | tf_op jit(solution)/shard_map/pallas_call | solution.py:47
  17.3 1.3 %shard_map.119 = f32[96,2048]{1,0:T(8,128)S(1)} custom-call(bf16[96,1792]{1,0:T(8,128)(2,1)S(1)} %constant_dynamic-update-slice_fusion.rows_ref.refs_0_, bf16[1792,2048]{1,0:T(8,128)(2,1)S(1)} %bitcast.15), custom_call_target="tpu_custom_call" | custom-call | flops 704643072 | bytes 1048576 | tf_op jit(solution)/shard_map/pallas_call | solution.py:47
  19.6 2.5 %collective-permute-start.7 = (bf16[24,1792]{1,0:T(8,128)(2,1)S(1)}, bf16[24,1792]{1,0:T(8,128)(2,1)S(1)}, u32[]{:S(2)}, u32[]{:S(2)}) collective-permute-start(bf16[24,1792]{1,0:T(8,128)(2,1)S(1)} %get-tuple-element.50), channel_id=1, source_target_pairs={{0,12},{4,8},{8,4},{12,0},{1,13},{5,9},{9,5},{13,1},{2,14},{6,10},... | collective-permute-start | bytes 258056 | tf_op jit(solution)/shard_map/ppermute | solution.py:21
  22.6 1.5 %collective-permute-start.5 = (bf16[24,1792]{1,0:T(8,128)(2,1)S(1)}, bf16[24,1792]{1,0:T(8,128)(2,1)S(1)}, u32[]{:S(2)}, u32[]{:S(2)}) collective-permute-start(bf16[24,1792]{1,0:T(8,128)(2,1)S(1)} %get-tuple-element.48), channel_id=1, source_target_pairs={{0,4},{4,0},{8,12},{12,8},{1,5},{5,1},{9,13},{13,9},{2,6},{6,2},{1... | collective-permute-start | bytes 258056 | tf_op jit(solution)/shard_map/ppermute | solution.py:21
  24.1 1.6 %collective-permute-start.8 = (bf16[96,1024]{1,0:T(8,128)(2,1)S(1)}, bf16[96,1024]{1,0:T(8,128)(2,1)S(1)}, u32[]{:S(2)}, u32[]{:S(2)}) collective-permute-start(bf16[96,1024]{1,0:T(8,128)(2,1)S(1)} %get-tuple-element.78), channel_id=1, source_target_pairs={{0,2},{1,3},{2,0},{3,1},{4,6},{5,7},{6,4},{7,5},{8,10},{9,11},{10,... | collective-permute-start | bytes 589832 | tf_op jit(solution)/shard_map/ppermute | solution.py:21
  26.7 3.9 %collective-permute-done.6 = bf16[24,1792]{1,0:T(8,128)(2,1)S(1)} collective-permute-done((bf16[24,1792]{1,0:T(8,128)(2,1)S(1)}, bf16[24,1792]{1,0:T(8,128)(2,1)S(1)}, u32[]{:S(2)}, u32[]{:S(2)}) %collective-permute-start.6) | collective-permute-done | bytes 86048 | tf_op jit(solution)/shard_map/ppermute | solution.py:21
  30.6 1.3 %shard_map.122 = f32[96,2048]{1,0:T(8,128)S(1)} custom-call(bf16[96,1792]{1,0:T(8,128)(2,1)S(1)} %pad_maximum_fusion.5.rows_ref.refs_0_, bf16[1792,2048]{1,0:T(8,128)(2,1)S(1)} %bitcast.13), custom_call_target="tpu_custom_call" | custom-call | flops 704643072 | bytes 1048576 | tf_op jit(solution)/shard_map/pallas_call | solution.py:47
  32.2 2.2 %collective-permute-done.9 = bf16[96,1024]{1,0:T(8,128)(2,1)S(1)} collective-permute-done((bf16[96,1024]{1,0:T(8,128)(2,1)S(1)}, bf16[96,1024]{1,0:T(8,128)(2,1)S(1)}, u32[]{:S(2)}, u32[]{:S(2)}) %collective-permute-start.9) | collective-permute-done | bytes 196640 | tf_op jit(solution)/shard_map/ppermute | solution.py:21
  34.7 1.6 %collective-permute-start.12 = (bf16[96,1024]{1,0:T(8,128)(2,1)S(1)}, bf16[96,1024]{1,0:T(8,128)(2,1)S(1)}, u32[]{:S(2)}, u32[]{:S(2)}) collective-permute-start(bf16[96,1024]{1,0:T(8,128)(2,1)S(1)} %get-tuple-element.72), channel_id=1, source_target_pairs={{0,2},{1,3},{2,0},{3,1},{4,6},{5,7},{6,4},{7,5},{8,10},{9,11},{10,... | collective-permute-start | bytes 589832 | tf_op jit(solution)/shard_map/ppermute | solution.py:21
  36.3 2.4 %convolution_convert_fusion = bf16[96,1792]{1,0:T(8,128)(2,1)S(1)} fusion(bf16[1792,2048]{1,0:T(8,128)(2,1)S(1)} %bitcast.13, bf16[96,1024]{1,0:T(8,128)(2,1)S(1)} %get-tuple-element.92, bf16[96,1024]{1,0:T(8,128)(2,1)S(1)} %get-tuple-element.91), kind=kOutput, calls=%fused_computation.1 | convolution fusion | flops 705601536 | bytes 8077312 | tf_op jit(solution)/shard_map/dot_general | solution.py:16
  38.8 3.4 %shard_map.123 = bf16[1792,2048]{1,0:T(8,128)(2,1)} custom-call(bf16[96,1792]{1,0:T(8,128)(2,1)S(1)} %pad_maximum_fusion.5.rows_ref.refs_0_, bf16[96,2048]{1,0:T(8,128)(2,1)S(1)} %pad_maximum_fusion.refs_1_), custom_call_target="tpu_custom_call" | custom-call | flops 704643072 | bytes 7340032 | tf_op jit(solution)/shard_map/pallas_call | solution.py:254
  43.7 1.3 %collective-permute-start.18 = (f32[96,1]{0,1:T(1,128)S(1)}, f32[96,1]{0,1:T(1,128)S(1)}, u32[]{:S(2)}, u32[]{:S(2)}) collective-permute-start(f32[96,1]{0,1:T(1,128)S(1)} %bitcast_add_fusion), channel_id=1, source_target_pairs={{0,2},{1,3},{2,0},{3,1},{4,6},{5,7},{6,4},{7,5},{8,10},{9,11},{10,... | collective-permute-start | bytes 1160 | tf_op jit(solution)/shard_map/ppermute | solution.py:21
  45.1 2.5 %collective-permute-start.16 = (bf16[24,1792]{1,0:T(8,128)(2,1)S(1)}, bf16[24,1792]{1,0:T(8,128)(2,1)S(1)}, u32[]{:S(2)}, u32[]{:S(2)}) collective-permute-start(bf16[24,1792]{1,0:T(8,128)(2,1)S(1)} %get-tuple-element.99), channel_id=1, source_target_pairs={{0,12},{4,8},{8,4},{12,0},{1,13},{5,9},{9,5},{13,1},{2,14},{6,10},... | collective-permute-start | bytes 258056 | tf_op jit(solution)/shard_map/ppermute | solution.py:21
  47.7 1.9 %collective-permute-start.14 = (bf16[24,1792]{1,0:T(8,128)(2,1)S(1)}, bf16[24,1792]{1,0:T(8,128)(2,1)S(1)}, u32[]{:S(2)}, u32[]{:S(2)}) collective-permute-start(bf16[24,1792]{1,0:T(8,128)(2,1)S(1)} %get-tuple-element.98), channel_id=1, source_target_pairs={{0,4},{4,0},{8,12},{12,8},{1,5},{5,1},{9,13},{13,9},{2,6},{6,2},{1... | collective-permute-start | bytes 258056 | tf_op jit(solution)/shard_map/ppermute | solution.py:21
  49.7 2.4 %fusion.8 = f32[96,1792]{1,0:T(8,128)S(1)} fusion(bf16[1792,2048]{1,0:T(8,128)(2,1)S(1)} %copy-done, bf16[96,1024]{1,0:T(8,128)(2,1)S(1)} %get-tuple-element.86, bf16[96,1024]{1,0:T(8,128)(2,1)S(1)} %get-tuple-element.85), kind=kOutput, calls=%fused_computation.55 | convolution fusion | flops 705429504 | bytes 8421376 | tf_op jit(solution)/shard_map/dot_general | solution.py:16
  52.2 2.5 %fusion = bf16[96,1792]{1,0:T(8,128)(2,1)S(1)} fusion(f32[96,1792]{1,0:T(8,128)S(1)} %fusion.8, bf16[1792,2048]{1,0:T(8,128)(2,1)S(1)} %bitcast.15, bf16[96,1024]{1,0:T(8,128)(2,1)S(1)} %get-tuple-element.89, bf16[96,1024]{1,0:T(8,128)(2,1)S(1)} %get-tuple-element.90), kind=kOutput, calls=%fused_computation.2 | convolution fusion | flops 705773568 | bytes 8765440 | tf_op jit(solution)/shard_map/dot_general | solution.py:16
  54.8 2.5 %collective-permute-start.21 = (bf16[24,1920]{1,0:T(8,128)(2,1)S(1)}, bf16[24,1920]{1,0:T(8,128)(2,1)S(1)}, u32[]{:S(2)}, u32[]{:S(2)}) collective-permute-start(bf16[24,1920]{1,0:T(8,128)(2,1)S(1)} %get-tuple-element.96), channel_id=1, source_target_pairs={{0,12},{4,8},{8,4},{12,0},{1,13},{5,9},{9,5},{13,1},{2,14},{6,10},... | collective-permute-start | bytes 276488 | tf_op jit(solution)/shard_map/ppermute | solution.py:21
  57.4 1.9 %collective-permute-start.19 = (bf16[24,1920]{1,0:T(8,128)(2,1)S(1)}, bf16[24,1920]{1,0:T(8,128)(2,1)S(1)}, u32[]{:S(2)}, u32[]{:S(2)}) collective-permute-start(bf16[24,1920]{1,0:T(8,128)(2,1)S(1)} %get-tuple-element.95), channel_id=1, source_target_pairs={{0,4},{4,0},{8,12},{12,8},{1,5},{5,1},{9,13},{13,9},{2,6},{6,2},{1... | collective-permute-start | bytes 276488 | tf_op jit(solution)/shard_map/ppermute | solution.py:21
  59.3 5.9 %shard_map.124 = (bf16[1792,2048]{1,0:T(8,128)(2,1)}, bf16[1792,2048]{1,0:T(8,128)(2,1)}, bf16[256,1792]{1,0:T(8,128)(2,1)}) custom-call(bf16[96,1792]{1,0:T(8,128)(2,1)S(1)} %constant_dynamic-update-slice_fusion.rows_ref.refs_0_, bf16[96,2048]{1,0:T(8,128)(2,1)S(1)} %get-tuple-element.104.refs_1_, bf16[96,2048]{1,0:T(8,128)(2,1)S(1)} %get-tuple-element.105.refs_2_, ...), custom_call_target="tpu_custom_call" | custom-call | flops 1409286144 | bytes 14680064 | tf_op jit(solution)/shard_map/pallas_call | solution.py:254
  65.3 2.4 %shard_map.125 = (bf16[256,1792]{1,0:T(8,128)(2,1)}, bf16[8,256]{1,0:T(8,128)(2,1)}) custom-call(s32[4]{0:T(128)S(1)} %iota_xor_fusion.labels_ref, s32[8,256]{1,0:T(8,128)S(1)} %bitcast.17, bf16[8,256]{1,0:T(8,128)(2,1)S(1)} %bitcast.19, bf16[96,256]{1,0:T(8,128)(2,1)S(1)} %get-tuple-element.66.pick_ref, bf16[96,1920]{1,0:T(8,128)(2,1)S(1)} %pad_maximum_fusion.4.back_ref), custom_call_target="tpu_custom_call" | custom-call | flops 1048576 | bytes 1048576 | tf_op jit(solution)/shard_map/pallas_call | solution.py:184
  (77 shorter events, 5.2 us)
Async XLA Ops:
  0.7 16.6 %slice-start.2 = ((s8[7340032]{0:T(1024)(128)(4,1)}), s8[4194304]{0:T(1024)(128)(4,1)S(1)}, s32[]{:S(2)}) async-start(s8[7340032]{0:T(1024)(128)(4,1)} %bitcast.14), calls=%async_computation.2 | async-start | bytes 8388608
  0.7 16.6 %slice-start.3 = ((s8[7340032]{0:T(1024)(128)(4,1)}), s8[3145728]{0:T(1024)(128)(4,1)S(1)}, s32[]{:S(2)}) async-start(s8[7340032]{0:T(1024)(128)(4,1)} %bitcast.14), calls=%async_computation.3 | async-start | bytes 6291456
  3.2 5.7 %collective-permute-start = (bf16[24,1792]{1,0:T(8,128)(2,1)S(1)}, bf16[24,1792]{1,0:T(8,128)(2,1)S(1)}, u32[]{:S(2)}, u32[]{:S(2)}) collective-permute-start(bf16[24,1792]{1,0:T(8,128)(2,1)S(1)} %get-tuple-element.42), channel_id=1, source_target_pairs={{0,4},{4,0},{8,12},{12,8},{1,5},{5,1},{9,13},{13,9},{2,6},{6,2},{1... | collective-permute-start | bytes 258056 | tf_op jit(solution)/shard_map/ppermute | solution.py:21
  6.2 9.5 %collective-permute-start.1 = (bf16[24,1792]{1,0:T(8,128)(2,1)S(1)}, bf16[24,1792]{1,0:T(8,128)(2,1)S(1)}, u32[]{:S(2)}, u32[]{:S(2)}) collective-permute-start(bf16[24,1792]{1,0:T(8,128)(2,1)S(1)} %get-tuple-element.43), channel_id=1, source_target_pairs={{0,8},{4,12},{8,0},{12,4},{1,9},{5,13},{9,1},{13,5},{2,10},{6,14},... | collective-permute-start | bytes 258056 | tf_op jit(solution)/shard_map/ppermute | solution.py:21
  8.8 6.9 %collective-permute-start.2 = (bf16[24,1792]{1,0:T(8,128)(2,1)S(1)}, bf16[24,1792]{1,0:T(8,128)(2,1)S(1)}, u32[]{:S(2)}, u32[]{:S(2)}) collective-permute-start(bf16[24,1792]{1,0:T(8,128)(2,1)S(1)} %get-tuple-element.44), channel_id=1, source_target_pairs={{0,12},{4,8},{8,4},{12,0},{1,13},{5,9},{9,5},{13,1},{2,14},{6,10},... | collective-permute-start | bytes 258056 | tf_op jit(solution)/shard_map/ppermute | solution.py:21
  17.2 2.0 %collective-permute-start.4 = (f32[96,1024]{1,0:T(8,128)S(1)}, f32[96,1024]{1,0:T(8,128)S(1)}, u32[]{:S(2)}, u32[]{:S(2)}) collective-permute-start(f32[96,1024]{1,0:T(8,128)S(1)} %slice_select_fusion.1), channel_id=1, source_target_pairs={{0,1},{1,0},{2,3},{3,2},{4,5},{5,4},{6,7},{7,6},{8,9},{9,8},{10,11... | collective-permute-start | bytes 1179656 | tf_op jit(solution)/shard_map/ppermute | solution.py:21
  18.6 5.4 %collective-permute-start.3 = (f32[96,1024]{1,0:T(8,128)S(1)}, f32[96,1024]{1,0:T(8,128)S(1)}, u32[]{:S(2)}, u32[]{:S(2)}) collective-permute-start(f32[96,1024]{1,0:T(8,128)S(1)} %slice_select_fusion.2), channel_id=1, source_target_pairs={{0,1},{1,0},{2,3},{3,2},{4,5},{5,4},{6,7},{7,6},{8,9},{9,8},{10,11... | collective-permute-start | bytes 1179656 | tf_op jit(solution)/shard_map/ppermute | solution.py:21
  19.6 7.1 %collective-permute-start.7 = (bf16[24,1792]{1,0:T(8,128)(2,1)S(1)}, bf16[24,1792]{1,0:T(8,128)(2,1)S(1)}, u32[]{:S(2)}, u32[]{:S(2)}) collective-permute-start(bf16[24,1792]{1,0:T(8,128)(2,1)S(1)} %get-tuple-element.50), channel_id=1, source_target_pairs={{0,12},{4,8},{8,4},{12,0},{1,13},{5,9},{9,5},{13,1},{2,14},{6,10},... | collective-permute-start | bytes 258056 | tf_op jit(solution)/shard_map/ppermute | solution.py:21
  22.1 8.4 %collective-permute-start.6 = (bf16[24,1792]{1,0:T(8,128)(2,1)S(1)}, bf16[24,1792]{1,0:T(8,128)(2,1)S(1)}, u32[]{:S(2)}, u32[]{:S(2)}) collective-permute-start(bf16[24,1792]{1,0:T(8,128)(2,1)S(1)} %get-tuple-element.49), channel_id=1, source_target_pairs={{0,8},{4,12},{8,0},{12,4},{1,9},{5,13},{9,1},{13,5},{2,10},{6,14},... | collective-permute-start | bytes 258056 | tf_op jit(solution)/shard_map/ppermute | solution.py:21
  22.6 8.0 %collective-permute-start.5 = (bf16[24,1792]{1,0:T(8,128)(2,1)S(1)}, bf16[24,1792]{1,0:T(8,128)(2,1)S(1)}, u32[]{:S(2)}, u32[]{:S(2)}) collective-permute-start(bf16[24,1792]{1,0:T(8,128)(2,1)S(1)} %get-tuple-element.48), channel_id=1, source_target_pairs={{0,4},{4,0},{8,12},{12,8},{1,5},{5,1},{9,13},{13,9},{2,6},{6,2},{1... | collective-permute-start | bytes 258056 | tf_op jit(solution)/shard_map/ppermute | solution.py:21
  24.1 7.9 %collective-permute-start.8 = (bf16[96,1024]{1,0:T(8,128)(2,1)S(1)}, bf16[96,1024]{1,0:T(8,128)(2,1)S(1)}, u32[]{:S(2)}, u32[]{:S(2)}) collective-permute-start(bf16[96,1024]{1,0:T(8,128)(2,1)S(1)} %get-tuple-element.78), channel_id=1, source_target_pairs={{0,2},{1,3},{2,0},{3,1},{4,6},{5,7},{6,4},{7,5},{8,10},{9,11},{10,... | collective-permute-start | bytes 589832 | tf_op jit(solution)/shard_map/ppermute | solution.py:21
  25.7 8.7 %collective-permute-start.9 = (bf16[96,1024]{1,0:T(8,128)(2,1)S(1)}, bf16[96,1024]{1,0:T(8,128)(2,1)S(1)}, u32[]{:S(2)}, u32[]{:S(2)}) collective-permute-start(bf16[96,1024]{1,0:T(8,128)(2,1)S(1)} %get-tuple-element.80), channel_id=1, source_target_pairs={{0,2},{1,3},{2,0},{3,1},{4,6},{5,7},{6,4},{7,5},{8,10},{9,11},{10,... | collective-permute-start | bytes 589832 | tf_op jit(solution)/shard_map/ppermute | solution.py:21
  32.0 2.6 %collective-permute-start.10 = (f32[96,1024]{1,0:T(8,128)S(1)}, f32[96,1024]{1,0:T(8,128)S(1)}, u32[]{:S(2)}, u32[]{:S(2)}) collective-permute-start(f32[96,1024]{1,0:T(8,128)S(1)} %slice_select_fusion), channel_id=1, source_target_pairs={{0,1},{1,0},{2,3},{3,2},{4,5},{5,4},{6,7},{7,6},{8,9},{9,8},{10,11... | collective-permute-start | bytes 1179656 | tf_op jit(solution)/shard_map/ppermute | solution.py:21
  34.6 1.6 %collective-permute-start.11 = (bf16[96,1024]{1,0:T(8,128)(2,1)S(1)}, bf16[96,1024]{1,0:T(8,128)(2,1)S(1)}, u32[]{:S(2)}, u32[]{:S(2)}) collective-permute-start(bf16[96,1024]{1,0:T(8,128)(2,1)S(1)} %get-tuple-element.54), channel_id=1, source_target_pairs={{0,1},{1,0},{2,3},{3,2},{4,5},{5,4},{6,7},{7,6},{8,9},{9,8},{10,11... | collective-permute-start | bytes 589832 | tf_op jit(solution)/shard_map/ppermute | solution.py:21
  34.7 7.5 %collective-permute-start.12 = (bf16[96,1024]{1,0:T(8,128)(2,1)S(1)}, bf16[96,1024]{1,0:T(8,128)(2,1)S(1)}, u32[]{:S(2)}, u32[]{:S(2)}) collective-permute-start(bf16[96,1024]{1,0:T(8,128)(2,1)S(1)} %get-tuple-element.72), channel_id=1, source_target_pairs={{0,2},{1,3},{2,0},{3,1},{4,6},{5,7},{6,4},{7,5},{8,10},{9,11},{10,... | collective-permute-start | bytes 589832 | tf_op jit(solution)/shard_map/ppermute | solution.py:21
  42.6 1.2 %collective-permute-start.17 = (f32[96,1]{0,1:T(1,128)S(1)}, f32[96,1]{0,1:T(1,128)S(1)}, u32[]{:S(2)}, u32[]{:S(2)}) collective-permute-start(f32[96,1]{0,1:T(1,128)S(1)} %bitcast.20), channel_id=1, source_target_pairs={{0,1},{1,0},{2,3},{3,2},{4,5},{5,4},{6,7},{7,6},{8,9},{9,8},{10,11... | collective-permute-start | bytes 1160 | tf_op jit(solution)/shard_map/ppermute | solution.py:21
  42.8 6.9 %collective-permute-start.13 = (bf16[96,2048]{1,0:T(8,128)(2,1)S(1)}, bf16[96,2048]{1,0:T(8,128)(2,1)S(1)}, u32[]{:S(2)}, u32[]{:S(2)}) collective-permute-start(bf16[96,2048]{1,0:T(8,128)(2,1)S(1)} %pad_maximum_fusion.1), channel_id=1, source_target_pairs={{0,1},{1,0},{2,3},{3,2},{4,5},{5,4},{6,7},{7,6},{8,9},{9,8},{10,11... | collective-permute-start | bytes 1179656 | tf_op jit(solution)/shard_map/ppermute | solution.py:21
  43.7 5.8 %collective-permute-start.18 = (f32[96,1]{0,1:T(1,128)S(1)}, f32[96,1]{0,1:T(1,128)S(1)}, u32[]{:S(2)}, u32[]{:S(2)}) collective-permute-start(f32[96,1]{0,1:T(1,128)S(1)} %bitcast_add_fusion), channel_id=1, source_target_pairs={{0,2},{1,3},{2,0},{3,1},{4,6},{5,7},{6,4},{7,5},{8,10},{9,11},{10,... | collective-permute-start | bytes 1160 | tf_op jit(solution)/shard_map/ppermute | solution.py:21
  45.1 12.2 %collective-permute-start.16 = (bf16[24,1792]{1,0:T(8,128)(2,1)S(1)}, bf16[24,1792]{1,0:T(8,128)(2,1)S(1)}, u32[]{:S(2)}, u32[]{:S(2)}) collective-permute-start(bf16[24,1792]{1,0:T(8,128)(2,1)S(1)} %get-tuple-element.99), channel_id=1, source_target_pairs={{0,12},{4,8},{8,4},{12,0},{1,13},{5,9},{9,5},{13,1},{2,14},{6,10},... | collective-permute-start | bytes 258056 | tf_op jit(solution)/shard_map/ppermute | solution.py:21
  47.7 11.6 %collective-permute-start.15 = (bf16[24,1792]{1,0:T(8,128)(2,1)S(1)}, bf16[24,1792]{1,0:T(8,128)(2,1)S(1)}, u32[]{:S(2)}, u32[]{:S(2)}) collective-permute-start(bf16[24,1792]{1,0:T(8,128)(2,1)S(1)} %get-tuple-element.100), channel_id=1, source_target_pairs={{0,8},{4,12},{8,0},{12,4},{1,9},{5,13},{9,1},{13,5},{2,10},{6,14},... | collective-permute-start | bytes 258056 | tf_op jit(solution)/shard_map/ppermute | solution.py:21
  47.7 11.6 %collective-permute-start.14 = (bf16[24,1792]{1,0:T(8,128)(2,1)S(1)}, bf16[24,1792]{1,0:T(8,128)(2,1)S(1)}, u32[]{:S(2)}, u32[]{:S(2)}) collective-permute-start(bf16[24,1792]{1,0:T(8,128)(2,1)S(1)} %get-tuple-element.98), channel_id=1, source_target_pairs={{0,4},{4,0},{8,12},{12,8},{1,5},{5,1},{9,13},{13,9},{2,6},{6,2},{1... | collective-permute-start | bytes 258056 | tf_op jit(solution)/shard_map/ppermute | solution.py:21
  54.8 10.4 %collective-permute-start.21 = (bf16[24,1920]{1,0:T(8,128)(2,1)S(1)}, bf16[24,1920]{1,0:T(8,128)(2,1)S(1)}, u32[]{:S(2)}, u32[]{:S(2)}) collective-permute-start(bf16[24,1920]{1,0:T(8,128)(2,1)S(1)} %get-tuple-element.96), channel_id=1, source_target_pairs={{0,12},{4,8},{8,4},{12,0},{1,13},{5,9},{9,5},{13,1},{2,14},{6,10},... | collective-permute-start | bytes 276488 | tf_op jit(solution)/shard_map/ppermute | solution.py:21
  57.3 7.9 %collective-permute-start.20 = (bf16[24,1920]{1,0:T(8,128)(2,1)S(1)}, bf16[24,1920]{1,0:T(8,128)(2,1)S(1)}, u32[]{:S(2)}, u32[]{:S(2)}) collective-permute-start(bf16[24,1920]{1,0:T(8,128)(2,1)S(1)} %get-tuple-element.97), channel_id=1, source_target_pairs={{0,8},{4,12},{8,0},{12,4},{1,9},{5,13},{9,1},{13,5},{2,10},{6,14},... | collective-permute-start | bytes 276488 | tf_op jit(solution)/shard_map/ppermute | solution.py:21
  57.4 7.9 %collective-permute-start.19 = (bf16[24,1920]{1,0:T(8,128)(2,1)S(1)}, bf16[24,1920]{1,0:T(8,128)(2,1)S(1)}, u32[]{:S(2)}, u32[]{:S(2)}) collective-permute-start(bf16[24,1920]{1,0:T(8,128)(2,1)S(1)} %get-tuple-element.95), channel_id=1, source_target_pairs={{0,4},{4,0},{8,12},{12,8},{1,5},{5,1},{9,13},{13,9},{2,6},{6,2},{1... | collective-permute-start | bytes 276488 | tf_op jit(solution)/shard_map/ppermute | solution.py:21
  (6 other events, 70.4 us)

commit v4 on v3

--- a/solution.py
+++ b/solution.py
@@ -212,6 +212,10 @@
     return total
 
 
+def shared_sum(total, got):
+    return lax.reduce_precision(total, 8, 7) + got.astype(F32)
+
+
 def join(values, even):
     half = values[0].shape[1]
     other = swap(jnp.concatenate(values, axis=1), "dp", 1)
@@ -301,6 +305,7 @@
     gate, up, grads = lax.optimization_barrier((gate, up, grads))
     hidden_grad = core_sum(project(grads, w_down), even)
     grad_swap = first_swap(hidden_grad)
+    even_gate, even_up = shared_sum(gate, gate_swap), shared_sum(up, up_swap)
     gate = chip_sum(gate, gate_swap)
     up = chip_sum(up, up_swap)
     sigma = jax.nn.sigmoid(gate)
@@ -309,6 +314,7 @@
         ((active * up).astype(BF), gate, up, sigma, active, hidden_grad))
     (hidden,) = join([hidden_h], even)
     part_out = dot(hidden, w_down, ((1,), (1,))).astype(BF)
+    even_grad = shared_sum(hidden_grad, grad_swap)
     hidden_grad = chip_sum(hidden_grad, grad_swap)
     d_up = (hidden_grad * active).astype(BF)
     d_gate = (hidden_grad * up * sigma * (1.0 + gate * (1.0 - sigma))).astype(BF)
@@ -316,10 +322,15 @@
     part_out, d_up, d_gate, grad_down = lax.optimization_barrier((part_out, d_up, d_gate, grad_down))
     back_out = exchange(cut(part_out), "expert") if direct else [move(cut(part_out))]
     d_up, d_gate = join([d_up, d_gate], even)
-    score = jnp.sum(hidden_grad * hidden_h.astype(F32), axis=1, keepdims=True)
+    pair = lax.axis_size("dp") == 4
+    if pair:
+        product = even_grad * (even_gate * jax.nn.sigmoid(even_gate) * even_up)
+    else:
+        product = hidden_grad * hidden_h.astype(F32)
+    score = jnp.sum(product, axis=1, keepdims=True)
     score = score + swap(score, "dp", 1)
     step = 2
-    while step < lax.axis_size("dp"):
+    while not pair and step < lax.axis_size("dp"):
         score = 0.5 * (score + swap(score, "dp", step))
         step *= 2
     high = lax.reduce_precision(score, 8, 7)

time: 68 us -> 66.2 us (0.974)
  starting transfers between devices: 25.4 us -> 24 us
    ppermute x22 -> x21, starting transfers between devices: 25.4 us -> 24 us  [swap(): return lax.ppermute(value, axis, [(i, i ^ step) for i in range(size)])]
    ppermute x22 -> x21, waiting for transfers between devices: 14 us -> 13.5 us  [swap(): return lax.ppermute(value, axis, [(i, i ^ step) for i in range(size)])]
  transfers between devices with their start and end apart: 22 -> 21, of which waited for: 5 -> 4; matrix products, arithmetic and copies ran while one was open for 12% -> 12% of each run, Pallas kernels for 18% -> 18%
where the time goes in v4:
time: 66.2 us; the launch traced here: 66.1 us
  starting transfers between devices  24 us (36%)
  Pallas kernels  18.4 us (28%)
  waiting for transfers between devices  13.5 us (20%)
  matrix products  7.3 us (11%)
  other arithmetic  1.59 us (2%)
  between operations  1.25 us (2%)
    ppermute x21, starting transfers between devices, swap(): return lax.ppermute(value, axis, [(i, i ^ step) for i in range(size)])  24 us
    ppermute x21, waiting for transfers between devices, swap(): return lax.ppermute(value, axis, [(i, i ^ step) for i in range(size)])  13.5 us
    pallas_call x2, Pallas kernels, weight_grads(): pl.pallas_call(body, in_specs=[vmem] * len(operands), out_specs=[pl.Block...  9.35 us
    dot_general x3, matrix products, dot(): lax.dot_general(left, right, (dims, ((), ())), preferred_element_type=F32)  7.3 us
    pallas_call x3, Pallas kernels, project(): pl.pallas_call(body, in_specs=[vmem, vmem], out_specs=vmem, out_shape=jax...  3.88 us
    pallas_call x1, Pallas kernels, route(): pl.pallas_call(body, in_specs=[pl.BlockSpec(memory_space=pltpu.SMEM)] + [...  2.46 us
    pallas_call x1, Pallas kernels, finish(): pl.pallas_call(body, in_specs=[pl.BlockSpec(memory_space=pltpu.SMEM)] + [...  2.38 us
  transfers between devices with their start and end apart: 21, of which 4 were waited for; matrix products, arithmetic and copies ran while one was open for 12% of the time, Pallas kernels for 18%

profile of v4, /device:TPU:0, one launch (start us, length us, event | category | flops | bytes accessed | tf_op | source)
XLA Modules:
  0.0 66.1 jit_solution(1202455939966905324)
XLA Ops:
  0.7 2.5 %shard_map.118 = (bf16[96,256]{1,0:T(8,128)(2,1)S(1)}, bf16[96,256]{1,0:T(8,128)(2,1)S(1)}, bf16[24,1792]{1,0:T(8,128)(2,1)S(1)}, bf16[24,1792]{1,0:T(8,128)(2,1...) custom-call(s32[4]{0:T(128)S(1)} %iota_xor_fusion.labels_ref, s32[8,256]{1,0:T(8,128)} %bitcast.17, ...), custom_call_target="tpu_custom_call" | custom-call | flops 17179869184 | bytes 1048576 | tf_op jit(solution)/shard_map/pallas_call | solution.py:120
  3.2 3.1 %collective-permute-start = (bf16[24,1792]{1,0:T(8,128)(2,1)S(1)}, bf16[24,1792]{1,0:T(8,128)(2,1)S(1)}, u32[]{:S(2)}, u32[]{:S(2)}) collective-permute-start(bf16[24,1792]{1,0:T(8,128)(2,1)S(1)} %get-tuple-element.42), channel_id=1, source_target_pairs={{0,4},{4,0},{8,12},{12,8},{1,5},{5,1},{9,13},{13,9},{2,6},{6,2},{1... | collective-permute-start | bytes 258056 | tf_op jit(solution)/shard_map/ppermute | solution.py:21
  6.2 2.6 %collective-permute-start.1 = (bf16[24,1792]{1,0:T(8,128)(2,1)S(1)}, bf16[24,1792]{1,0:T(8,128)(2,1)S(1)}, u32[]{:S(2)}, u32[]{:S(2)}) collective-permute-start(bf16[24,1792]{1,0:T(8,128)(2,1)S(1)} %get-tuple-element.43), channel_id=1, source_target_pairs={{0,8},{4,12},{8,0},{12,4},{1,9},{5,13},{9,1},{13,5},{2,10},{6,14},... | collective-permute-start | bytes 258056 | tf_op jit(solution)/shard_map/ppermute | solution.py:21
  8.9 6.9 %collective-permute-done.1 = bf16[24,1792]{1,0:T(8,128)(2,1)S(1)} collective-permute-done((bf16[24,1792]{1,0:T(8,128)(2,1)S(1)}, bf16[24,1792]{1,0:T(8,128)(2,1)S(1)}, u32[]{:S(2)}, u32[]{:S(2)}) %collective-permute-start.1) | collective-permute-done | bytes 86048 | tf_op jit(solution)/shard_map/ppermute | solution.py:21
  15.8 1.3 %shard_map.120 = f32[96,2048]{1,0:T(8,128)S(1)} custom-call(bf16[96,1792]{1,0:T(8,128)(2,1)S(1)} %constant_dynamic-update-slice_fusion.rows_ref.refs_0_, bf16[1792,2048]{1,0:T(8,128)(2,1)S(1)} %copy-done), custom_call_target="tpu_custom_call" | custom-call | flops 704643072 | bytes 1048576 | tf_op jit(solution)/shard_map/pallas_call | solution.py:47
  17.3 1.3 %shard_map.119 = f32[96,2048]{1,0:T(8,128)S(1)} custom-call(bf16[96,1792]{1,0:T(8,128)(2,1)S(1)} %constant_dynamic-update-slice_fusion.rows_ref.refs_0_, bf16[1792,2048]{1,0:T(8,128)(2,1)S(1)} %bitcast.16), custom_call_target="tpu_custom_call" | custom-call | flops 704643072 | bytes 1048576 | tf_op jit(solution)/shard_map/pallas_call | solution.py:47
  18.6 0.5 collective-permute-start.3
  19.6 2.5 %collective-permute-start.7 = (bf16[24,1792]{1,0:T(8,128)(2,1)S(1)}, bf16[24,1792]{1,0:T(8,128)(2,1)S(1)}, u32[]{:S(2)}, u32[]{:S(2)}) collective-permute-start(bf16[24,1792]{1,0:T(8,128)(2,1)S(1)} %get-tuple-element.50), channel_id=1, source_target_pairs={{0,12},{4,8},{8,4},{12,0},{1,13},{5,9},{9,5},{13,1},{2,14},{6,10},... | collective-permute-start | bytes 258056 | tf_op jit(solution)/shard_map/ppermute | solution.py:21
  22.6 1.5 %collective-permute-start.5 = (bf16[24,1792]{1,0:T(8,128)(2,1)S(1)}, bf16[24,1792]{1,0:T(8,128)(2,1)S(1)}, u32[]{:S(2)}, u32[]{:S(2)}) collective-permute-start(bf16[24,1792]{1,0:T(8,128)(2,1)S(1)} %get-tuple-element.48), channel_id=1, source_target_pairs={{0,4},{4,0},{8,12},{12,8},{1,5},{5,1},{9,13},{13,9},{2,6},{6,2},{1... | collective-permute-start | bytes 258056 | tf_op jit(solution)/shard_map/ppermute | solution.py:21
  24.1 1.6 %collective-permute-start.8 = (bf16[96,1024]{1,0:T(8,128)(2,1)S(1)}, bf16[96,1024]{1,0:T(8,128)(2,1)S(1)}, u32[]{:S(2)}, u32[]{:S(2)}) collective-permute-start(bf16[96,1024]{1,0:T(8,128)(2,1)S(1)} %get-tuple-element.78), channel_id=1, source_target_pairs={{0,2},{1,3},{2,0},{3,1},{4,6},{5,7},{6,4},{7,5},{8,10},{9,11},{10,... | collective-permute-start | bytes 589832 | tf_op jit(solution)/shard_map/ppermute | solution.py:21
  26.7 3.9 %collective-permute-done.6 = bf16[24,1792]{1,0:T(8,128)(2,1)S(1)} collective-permute-done((bf16[24,1792]{1,0:T(8,128)(2,1)S(1)}, bf16[24,1792]{1,0:T(8,128)(2,1)S(1)}, u32[]{:S(2)}, u32[]{:S(2)}) %collective-permute-start.6) | collective-permute-done | bytes 86048 | tf_op jit(solution)/shard_map/ppermute | solution.py:21
  30.6 1.3 %shard_map.122 = f32[96,2048]{1,0:T(8,128)S(1)} custom-call(bf16[96,1792]{1,0:T(8,128)(2,1)S(1)} %pad_maximum_fusion.5.rows_ref.refs_0_, bf16[1792,2048]{1,0:T(8,128)(2,1)S(1)} %bitcast.14), custom_call_target="tpu_custom_call" | custom-call | flops 704643072 | bytes 1048576 | tf_op jit(solution)/shard_map/pallas_call | solution.py:47
  32.2 2.2 %collective-permute-done.9 = bf16[96,1024]{1,0:T(8,128)(2,1)S(1)} collective-permute-done((bf16[96,1024]{1,0:T(8,128)(2,1)S(1)}, bf16[96,1024]{1,0:T(8,128)(2,1)S(1)}, u32[]{:S(2)}, u32[]{:S(2)}) %collective-permute-start.9) | collective-permute-done | bytes 196640 | tf_op jit(solution)/shard_map/ppermute | solution.py:21
  34.7 1.6 %collective-permute-start.12 = (bf16[96,1024]{1,0:T(8,128)(2,1)S(1)}, bf16[96,1024]{1,0:T(8,128)(2,1)S(1)}, u32[]{:S(2)}, u32[]{:S(2)}) collective-permute-start(bf16[96,1024]{1,0:T(8,128)(2,1)S(1)} %get-tuple-element.72), channel_id=1, source_target_pairs={{0,2},{1,3},{2,0},{3,1},{4,6},{5,7},{6,4},{7,5},{8,10},{9,11},{10,... | collective-permute-start | bytes 589832 | tf_op jit(solution)/shard_map/ppermute | solution.py:21
  36.3 2.4 %convolution_convert_fusion = bf16[96,1792]{1,0:T(8,128)(2,1)S(1)} fusion(bf16[1792,2048]{1,0:T(8,128)(2,1)S(1)} %bitcast.14, bf16[96,1024]{1,0:T(8,128)(2,1)S(1)} %get-tuple-element.92, bf16[96,1024]{1,0:T(8,128)(2,1)S(1)} %get-tuple-element.91), kind=kOutput, calls=%fused_computation.1 | convolution fusion | flops 705601536 | bytes 8077312 | tf_op jit(solution)/shard_map/dot_general | solution.py:16
  38.7 3.4 %shard_map.123 = bf16[1792,2048]{1,0:T(8,128)(2,1)} custom-call(bf16[96,1792]{1,0:T(8,128)(2,1)S(1)} %pad_maximum_fusion.5.rows_ref.refs_0_, bf16[96,2048]{1,0:T(8,128)(2,1)S(1)} %pad_maximum_fusion.refs_1_), custom_call_target="tpu_custom_call" | custom-call | flops 704643072 | bytes 7340032 | tf_op jit(solution)/shard_map/pallas_call | solution.py:258
  43.3 2.5 %collective-permute-start.16 = (bf16[24,1792]{1,0:T(8,128)(2,1)S(1)}, bf16[24,1792]{1,0:T(8,128)(2,1)S(1)}, u32[]{:S(2)}, u32[]{:S(2)}) collective-permute-start(bf16[24,1792]{1,0:T(8,128)(2,1)S(1)} %get-tuple-element.99), channel_id=1, source_target_pairs={{0,12},{4,8},{8,4},{12,0},{1,13},{5,9},{9,5},{13,1},{2,14},{6,10},... | collective-permute-start | bytes 258056 | tf_op jit(solution)/shard_map/ppermute | solution.py:21
  45.9 1.9 %collective-permute-start.14 = (bf16[24,1792]{1,0:T(8,128)(2,1)S(1)}, bf16[24,1792]{1,0:T(8,128)(2,1)S(1)}, u32[]{:S(2)}, u32[]{:S(2)}) collective-permute-start(bf16[24,1792]{1,0:T(8,128)(2,1)S(1)} %get-tuple-element.98), channel_id=1, source_target_pairs={{0,4},{4,0},{8,12},{12,8},{1,5},{5,1},{9,13},{13,9},{2,6},{6,2},{1... | collective-permute-start | bytes 258056 | tf_op jit(solution)/shard_map/ppermute | solution.py:21
  48.0 2.4 %fusion.11 = f32[96,1792]{1,0:T(8,128)S(1)} fusion(bf16[1792,2048]{1,0:T(8,128)(2,1)S(1)} %copy-done, bf16[96,1024]{1,0:T(8,128)(2,1)S(1)} %get-tuple-element.86, bf16[96,1024]{1,0:T(8,128)(2,1)S(1)} %get-tuple-element.85), kind=kOutput, calls=%fused_computation.58 | convolution fusion | flops 705429504 | bytes 8421376 | tf_op jit(solution)/shard_map/dot_general | solution.py:16
  50.4 2.6 %fusion = bf16[96,1792]{1,0:T(8,128)(2,1)S(1)} fusion(f32[96,1792]{1,0:T(8,128)S(1)} %fusion.11, bf16[1792,2048]{1,0:T(8,128)(2,1)S(1)} %bitcast.16, bf16[96,1024]{1,0:T(8,128)(2,1)S(1)} %get-tuple-element.89, bf16[96,1024]{1,0:T(8,128)(2,1)S(1)} %get-tuple-element.90), kind=kOutput, calls=%fused_computation.2 | convolution fusion | flops 705773568 | bytes 8765440 | tf_op jit(solution)/shard_map/dot_general | solution.py:16
  53.1 2.5 %collective-permute-start.20 = (bf16[24,1920]{1,0:T(8,128)(2,1)S(1)}, bf16[24,1920]{1,0:T(8,128)(2,1)S(1)}, u32[]{:S(2)}, u32[]{:S(2)}) collective-permute-start(bf16[24,1920]{1,0:T(8,128)(2,1)S(1)} %get-tuple-element.96), channel_id=1, source_target_pairs={{0,12},{4,8},{8,4},{12,0},{1,13},{5,9},{9,5},{13,1},{2,14},{6,10},... | collective-permute-start | bytes 276488 | tf_op jit(solution)/shard_map/ppermute | solution.py:21
  55.6 1.9 %collective-permute-start.18 = (bf16[24,1920]{1,0:T(8,128)(2,1)S(1)}, bf16[24,1920]{1,0:T(8,128)(2,1)S(1)}, u32[]{:S(2)}, u32[]{:S(2)}) collective-permute-start(bf16[24,1920]{1,0:T(8,128)(2,1)S(1)} %get-tuple-element.95), channel_id=1, source_target_pairs={{0,4},{4,0},{8,12},{12,8},{1,5},{5,1},{9,13},{13,9},{2,6},{6,2},{1... | collective-permute-start | bytes 276488 | tf_op jit(solution)/shard_map/ppermute | solution.py:21
  57.5 5.9 %shard_map.124 = (bf16[1792,2048]{1,0:T(8,128)(2,1)}, bf16[1792,2048]{1,0:T(8,128)(2,1)}, bf16[256,1792]{1,0:T(8,128)(2,1)}) custom-call(bf16[96,1792]{1,0:T(8,128)(2,1)S(1)} %constant_dynamic-update-slice_fusion.rows_ref.refs_0_, bf16[96,2048]{1,0:T(8,128)(2,1)S(1)} %get-tuple-element.104.refs_1_, bf16[96,2048]{1,0:T(8,128)(2,1)S(1)} %get-tuple-element.105.refs_2_, ...), custom_call_target="tpu_custom_call" | custom-call | flops 1409286144 | bytes 14680064 | tf_op jit(solution)/shard_map/pallas_call | solution.py:258
  63.6 2.4 %shard_map.125 = (bf16[256,1792]{1,0:T(8,128)(2,1)}, bf16[8,256]{1,0:T(8,128)(2,1)}) custom-call(s32[4]{0:T(128)S(1)} %iota_xor_fusion.labels_ref, s32[8,256]{1,0:T(8,128)S(1)} %bitcast.18, bf16[8,256]{1,0:T(8,128)(2,1)S(1)} %bitcast.20, bf16[96,256]{1,0:T(8,128)(2,1)S(1)} %get-tuple-element.66.pick_ref, bf16[96,1920]{1,0:T(8,128)(2,1)S(1)} %pad_maximum_fusion.4.back_ref), custom_call_target="tpu_custom_call" | custom-call | flops 1048576 | bytes 1048576 | tf_op jit(solution)/shard_map/pallas_call | solution.py:184
  (74 shorter events, 4.3 us)
Async XLA Ops:
  0.7 16.6 %slice-start.2 = ((s8[7340032]{0:T(1024)(128)(4,1)}), s8[4194304]{0:T(1024)(128)(4,1)S(1)}, s32[]{:S(2)}) async-start(s8[7340032]{0:T(1024)(128)(4,1)} %bitcast.15), calls=%async_computation.2 | async-start | bytes 8388608
  0.7 15.1 %copy-start = (bf16[1792,2048]{1,0:T(8,128)(2,1)S(1)}, bf16[1792,2048]{1,0:T(8,128)(2,1)}, u32[]{:S(2)}) copy-start(bf16[1792,2048]{1,0:T(8,128)(2,1)} %weight_ref.4) | copy-start | bytes 22020100
  0.7 16.6 %slice-start.3 = ((s8[7340032]{0:T(1024)(128)(4,1)}), s8[3145728]{0:T(1024)(128)(4,1)S(1)}, s32[]{:S(2)}) async-start(s8[7340032]{0:T(1024)(128)(4,1)} %bitcast.15), calls=%async_computation.3 | async-start | bytes 6291456
  3.2 5.7 %collective-permute-start = (bf16[24,1792]{1,0:T(8,128)(2,1)S(1)}, bf16[24,1792]{1,0:T(8,128)(2,1)S(1)}, u32[]{:S(2)}, u32[]{:S(2)}) collective-permute-start(bf16[24,1792]{1,0:T(8,128)(2,1)S(1)} %get-tuple-element.42), channel_id=1, source_target_pairs={{0,4},{4,0},{8,12},{12,8},{1,5},{5,1},{9,13},{13,9},{2,6},{6,2},{1... | collective-permute-start | bytes 258056 | tf_op jit(solution)/shard_map/ppermute | solution.py:21
  6.2 9.5 %collective-permute-start.1 = (bf16[24,1792]{1,0:T(8,128)(2,1)S(1)}, bf16[24,1792]{1,0:T(8,128)(2,1)S(1)}, u32[]{:S(2)}, u32[]{:S(2)}) collective-permute-start(bf16[24,1792]{1,0:T(8,128)(2,1)S(1)} %get-tuple-element.43), channel_id=1, source_target_pairs={{0,8},{4,12},{8,0},{12,4},{1,9},{5,13},{9,1},{13,5},{2,10},{6,14},... | collective-permute-start | bytes 258056 | tf_op jit(solution)/shard_map/ppermute | solution.py:21
  8.8 6.9 %collective-permute-start.2 = (bf16[24,1792]{1,0:T(8,128)(2,1)S(1)}, bf16[24,1792]{1,0:T(8,128)(2,1)S(1)}, u32[]{:S(2)}, u32[]{:S(2)}) collective-permute-start(bf16[24,1792]{1,0:T(8,128)(2,1)S(1)} %get-tuple-element.44), channel_id=1, source_target_pairs={{0,12},{4,8},{8,4},{12,0},{1,13},{5,9},{9,5},{13,1},{2,14},{6,10},... | collective-permute-start | bytes 258056 | tf_op jit(solution)/shard_map/ppermute | solution.py:21
  17.2 2.0 %collective-permute-start.4 = (f32[96,1024]{1,0:T(8,128)S(1)}, f32[96,1024]{1,0:T(8,128)S(1)}, u32[]{:S(2)}, u32[]{:S(2)}) collective-permute-start(f32[96,1024]{1,0:T(8,128)S(1)} %slice_select_fusion.1), channel_id=1, source_target_pairs={{0,1},{1,0},{2,3},{3,2},{4,5},{5,4},{6,7},{7,6},{8,9},{9,8},{10,11... | collective-permute-start | bytes 1179656 | tf_op jit(solution)/shard_map/ppermute | solution.py:21
  18.6 5.4 %collective-permute-start.3 = (f32[96,1024]{1,0:T(8,128)S(1)}, f32[96,1024]{1,0:T(8,128)S(1)}, u32[]{:S(2)}, u32[]{:S(2)}) collective-permute-start(f32[96,1024]{1,0:T(8,128)S(1)} %slice_select_fusion.2), channel_id=1, source_target_pairs={{0,1},{1,0},{2,3},{3,2},{4,5},{5,4},{6,7},{7,6},{8,9},{9,8},{10,11... | collective-permute-start | bytes 1179656 | tf_op jit(solution)/shard_map/ppermute | solution.py:21
  19.6 7.1 %collective-permute-start.7 = (bf16[24,1792]{1,0:T(8,128)(2,1)S(1)}, bf16[24,1792]{1,0:T(8,128)(2,1)S(1)}, u32[]{:S(2)}, u32[]{:S(2)}) collective-permute-start(bf16[24,1792]{1,0:T(8,128)(2,1)S(1)} %get-tuple-element.50), channel_id=1, source_target_pairs={{0,12},{4,8},{8,4},{12,0},{1,13},{5,9},{9,5},{13,1},{2,14},{6,10},... | collective-permute-start | bytes 258056 | tf_op jit(solution)/shard_map/ppermute | solution.py:21
  22.1 8.4 %collective-permute-start.6 = (bf16[24,1792]{1,0:T(8,128)(2,1)S(1)}, bf16[24,1792]{1,0:T(8,128)(2,1)S(1)}, u32[]{:S(2)}, u32[]{:S(2)}) collective-permute-start(bf16[24,1792]{1,0:T(8,128)(2,1)S(1)} %get-tuple-element.49), channel_id=1, source_target_pairs={{0,8},{4,12},{8,0},{12,4},{1,9},{5,13},{9,1},{13,5},{2,10},{6,14},... | collective-permute-start | bytes 258056 | tf_op jit(solution)/shard_map/ppermute | solution.py:21
  22.6 8.0 %collective-permute-start.5 = (bf16[24,1792]{1,0:T(8,128)(2,1)S(1)}, bf16[24,1792]{1,0:T(8,128)(2,1)S(1)}, u32[]{:S(2)}, u32[]{:S(2)}) collective-permute-start(bf16[24,1792]{1,0:T(8,128)(2,1)S(1)} %get-tuple-element.48), channel_id=1, source_target_pairs={{0,4},{4,0},{8,12},{12,8},{1,5},{5,1},{9,13},{13,9},{2,6},{6,2},{1... | collective-permute-start | bytes 258056 | tf_op jit(solution)/shard_map/ppermute | solution.py:21
  24.1 7.9 %collective-permute-start.8 = (bf16[96,1024]{1,0:T(8,128)(2,1)S(1)}, bf16[96,1024]{1,0:T(8,128)(2,1)S(1)}, u32[]{:S(2)}, u32[]{:S(2)}) collective-permute-start(bf16[96,1024]{1,0:T(8,128)(2,1)S(1)} %get-tuple-element.78), channel_id=1, source_target_pairs={{0,2},{1,3},{2,0},{3,1},{4,6},{5,7},{6,4},{7,5},{8,10},{9,11},{10,... | collective-permute-start | bytes 589832 | tf_op jit(solution)/shard_map/ppermute | solution.py:21
  25.7 8.7 %collective-permute-start.9 = (bf16[96,1024]{1,0:T(8,128)(2,1)S(1)}, bf16[96,1024]{1,0:T(8,128)(2,1)S(1)}, u32[]{:S(2)}, u32[]{:S(2)}) collective-permute-start(bf16[96,1024]{1,0:T(8,128)(2,1)S(1)} %get-tuple-element.80), channel_id=1, source_target_pairs={{0,2},{1,3},{2,0},{3,1},{4,6},{5,7},{6,4},{7,5},{8,10},{9,11},{10,... | collective-permute-start | bytes 589832 | tf_op jit(solution)/shard_map/ppermute | solution.py:21
  31.9 2.6 %collective-permute-start.10 = (f32[96,1024]{1,0:T(8,128)S(1)}, f32[96,1024]{1,0:T(8,128)S(1)}, u32[]{:S(2)}, u32[]{:S(2)}) collective-permute-start(f32[96,1024]{1,0:T(8,128)S(1)} %slice_select_fusion), channel_id=1, source_target_pairs={{0,1},{1,0},{2,3},{3,2},{4,5},{5,4},{6,7},{7,6},{8,9},{9,8},{10,11... | collective-permute-start | bytes 1179656 | tf_op jit(solution)/shard_map/ppermute | solution.py:21
  34.6 1.6 %collective-permute-start.11 = (bf16[96,1024]{1,0:T(8,128)(2,1)S(1)}, bf16[96,1024]{1,0:T(8,128)(2,1)S(1)}, u32[]{:S(2)}, u32[]{:S(2)}) collective-permute-start(bf16[96,1024]{1,0:T(8,128)(2,1)S(1)} %get-tuple-element.54), channel_id=1, source_target_pairs={{0,1},{1,0},{2,3},{3,2},{4,5},{5,4},{6,7},{7,6},{8,9},{9,8},{10,11... | collective-permute-start | bytes 589832 | tf_op jit(solution)/shard_map/ppermute | solution.py:21
  34.7 7.5 %collective-permute-start.12 = (bf16[96,1024]{1,0:T(8,128)(2,1)S(1)}, bf16[96,1024]{1,0:T(8,128)(2,1)S(1)}, u32[]{:S(2)}, u32[]{:S(2)}) collective-permute-start(bf16[96,1024]{1,0:T(8,128)(2,1)S(1)} %get-tuple-element.72), channel_id=1, source_target_pairs={{0,2},{1,3},{2,0},{3,1},{4,6},{5,7},{6,4},{7,5},{8,10},{9,11},{10,... | collective-permute-start | bytes 589832 | tf_op jit(solution)/shard_map/ppermute | solution.py:21
  42.7 5.2 %collective-permute-start.13 = (bf16[96,2048]{1,0:T(8,128)(2,1)S(1)}, bf16[96,2048]{1,0:T(8,128)(2,1)S(1)}, u32[]{:S(2)}, u32[]{:S(2)}) collective-permute-start(bf16[96,2048]{1,0:T(8,128)(2,1)S(1)} %pad_maximum_fusion.1), channel_id=1, source_target_pairs={{0,1},{1,0},{2,3},{3,2},{4,5},{5,4},{6,7},{7,6},{8,9},{9,8},{10,11... | collective-permute-start | bytes 1179656 | tf_op jit(solution)/shard_map/ppermute | solution.py:21
  43.0 4.8 %collective-permute-start.17 = (f32[96,1]{0,1:T(1,128)S(1)}, f32[96,1]{0,1:T(1,128)S(1)}, u32[]{:S(2)}, u32[]{:S(2)}) collective-permute-start(f32[96,1]{0,1:T(1,128)S(1)} %bitcast.21), channel_id=1, source_target_pairs={{0,1},{1,0},{2,3},{3,2},{4,5},{5,4},{6,7},{7,6},{8,9},{9,8},{10,11... | collective-permute-start | bytes 1160 | tf_op jit(solution)/shard_map/ppermute | solution.py:21
  43.3 12.3 %collective-permute-start.16 = (bf16[24,1792]{1,0:T(8,128)(2,1)S(1)}, bf16[24,1792]{1,0:T(8,128)(2,1)S(1)}, u32[]{:S(2)}, u32[]{:S(2)}) collective-permute-start(bf16[24,1792]{1,0:T(8,128)(2,1)S(1)} %get-tuple-element.99), channel_id=1, source_target_pairs={{0,12},{4,8},{8,4},{12,0},{1,13},{5,9},{9,5},{13,1},{2,14},{6,10},... | collective-permute-start | bytes 258056 | tf_op jit(solution)/shard_map/ppermute | solution.py:21
  45.9 11.6 %collective-permute-start.15 = (bf16[24,1792]{1,0:T(8,128)(2,1)S(1)}, bf16[24,1792]{1,0:T(8,128)(2,1)S(1)}, u32[]{:S(2)}, u32[]{:S(2)}) collective-permute-start(bf16[24,1792]{1,0:T(8,128)(2,1)S(1)} %get-tuple-element.100), channel_id=1, source_target_pairs={{0,8},{4,12},{8,0},{12,4},{1,9},{5,13},{9,1},{13,5},{2,10},{6,14},... | collective-permute-start | bytes 258056 | tf_op jit(solution)/shard_map/ppermute | solution.py:21
  45.9 11.6 %collective-permute-start.14 = (bf16[24,1792]{1,0:T(8,128)(2,1)S(1)}, bf16[24,1792]{1,0:T(8,128)(2,1)S(1)}, u32[]{:S(2)}, u32[]{:S(2)}) collective-permute-start(bf16[24,1792]{1,0:T(8,128)(2,1)S(1)} %get-tuple-element.98), channel_id=1, source_target_pairs={{0,4},{4,0},{8,12},{12,8},{1,5},{5,1},{9,13},{13,9},{2,6},{6,2},{1... | collective-permute-start | bytes 258056 | tf_op jit(solution)/shard_map/ppermute | solution.py:21
  53.1 10.4 %collective-permute-start.20 = (bf16[24,1920]{1,0:T(8,128)(2,1)S(1)}, bf16[24,1920]{1,0:T(8,128)(2,1)S(1)}, u32[]{:S(2)}, u32[]{:S(2)}) collective-permute-start(bf16[24,1920]{1,0:T(8,128)(2,1)S(1)} %get-tuple-element.96), channel_id=1, source_target_pairs={{0,12},{4,8},{8,4},{12,0},{1,13},{5,9},{9,5},{13,1},{2,14},{6,10},... | collective-permute-start | bytes 276488 | tf_op jit(solution)/shard_map/ppermute | solution.py:21
  55.6 7.9 %collective-permute-start.19 = (bf16[24,1920]{1,0:T(8,128)(2,1)S(1)}, bf16[24,1920]{1,0:T(8,128)(2,1)S(1)}, u32[]{:S(2)}, u32[]{:S(2)}) collective-permute-start(bf16[24,1920]{1,0:T(8,128)(2,1)S(1)} %get-tuple-element.97), channel_id=1, source_target_pairs={{0,8},{4,12},{8,0},{12,4},{1,9},{5,13},{9,1},{13,5},{2,10},{6,14},... | collective-permute-start | bytes 276488 | tf_op jit(solution)/shard_map/ppermute | solution.py:21
  55.6 7.9 %collective-permute-start.18 = (bf16[24,1920]{1,0:T(8,128)(2,1)S(1)}, bf16[24,1920]{1,0:T(8,128)(2,1)S(1)}, u32[]{:S(2)}, u32[]{:S(2)}) collective-permute-start(bf16[24,1920]{1,0:T(8,128)(2,1)S(1)} %get-tuple-element.95), channel_id=1, source_target_pairs={{0,4},{4,0},{8,12},{12,8},{1,5},{5,1},{9,13},{13,9},{2,6},{6,2},{1... | collective-permute-start | bytes 276488 | tf_op jit(solution)/shard_map/ppermute | solution.py:21
  (5 other events, 55.3 us)
